TPU v7x, 32 devices: a whole 2x2x4 slice. The times are simulated.
32 devices in a mesh: dp: 4 (over z), seq: 4 (over x, core), blk: 2 (over y).
Axes of the slice: x: 2, y: 2, z: 4, core: 2. Of those that a mesh axis runs over, the one named last changes fastest.
Arguments:
- tokens: bfloat16 [4096, 768], P(('dp', 'seq', 'blk')), may hold values from -6 to 6
- cotangent: bfloat16 [4096, 768], P(('dp', 'seq', 'blk')), may hold values from -6 to 6
- qkv_weight: float32 [768, 2304], P(('dp', 'seq', 'blk')), may hold values from -0.21875 to 0.21875
- proj_weight: float32 [768, 768], P(('dp', 'seq', 'blk')), may hold values from -0.625 to 0.625
- expand_weight: float32 [768, 3072], P(('dp', 'seq', 'blk')), may hold values from -0.21875 to 0.21875
- shrink_weight: float32 [3072, 768], P(('dp', 'seq', 'blk')), may hold values from -0.109375 to 0.109375
- small_params: float32 [12, 768], P(None, ('dp', 'seq', 'blk')), may hold values from -0.6 to 1.5, as said below
- qkv_first: float32 [768, 2304], P(('dp', 'seq', 'blk')), may hold values from -12 to 12
- proj_first: float32 [768, 768], P(('dp', 'seq', 'blk')), may hold values from -12 to 12
- expand_first: float32 [768, 3072], P(('dp', 'seq', 'blk')), may hold values from -16 to 16
- shrink_first: float32 [3072, 768], P(('dp', 'seq', 'blk')), may hold values from -24 to 24
- small_first: float32 [12, 768], P(None, ('dp', 'seq', 'blk')), may hold values from -20 to 20
- qkv_second: float32 [768, 2304], P(('dp', 'seq', 'blk')), may hold values from 19.6608 to 77.824
- proj_second: float32 [768, 768], P(('dp', 'seq', 'blk')), may hold values from 19.6608 to 77.824
- expand_second: float32 [768, 3072], P(('dp', 'seq', 'blk')), may hold values from 26.624 to 106.496
- shrink_second: float32 [3072, 768], P(('dp', 'seq', 'blk')), may hold values from 77.824 to 311.296
- small_second: float32 [12, 768], P(None, ('dp', 'seq', 'blk')), may hold values from 53.248 to 217.088
Outputs:
- block_out: float32 [4096, 768], P(('dp', 'seq', 'blk'))
- token_grad: float32 [4096, 768], P(('dp', 'seq', 'blk'))
- qkv_moment: float32 [768, 2304], P(('dp', 'seq', 'blk'))
- qkv_variance: float32 [768, 2304], P(('dp', 'seq', 'blk'))
- qkv_updated: float32 [768, 2304], P(('dp', 'seq', 'blk'))
- proj_moment: float32 [768, 768], P(('dp', 'seq', 'blk'))
- proj_variance: float32 [768, 768], P(('dp', 'seq', 'blk'))
- proj_updated: float32 [768, 768], P(('dp', 'seq', 'blk'))
- expand_moment: float32 [768, 3072], P(('dp', 'seq', 'blk'))
- expand_variance: float32 [768, 3072], P(('dp', 'seq', 'blk'))
- expand_updated: float32 [768, 3072], P(('dp', 'seq', 'blk'))
- shrink_moment: float32 [3072, 768], P(('dp', 'seq', 'blk'))
- shrink_variance: float32 [3072, 768], P(('dp', 'seq', 'blk'))
- shrink_updated: float32 [3072, 768], P(('dp', 'seq', 'blk'))
- small_moment: float32 [12, 768], P(None, ('dp', 'seq', 'blk'))
- small_variance: float32 [12, 768], P(None, ('dp', 'seq', 'blk'))
- small_updated: float32 [12, 768], P(None, ('dp', 'seq', 'blk'))
Inputs may be any that keep to these rules, and one draw needn't show every extreme that they name: `small_params`: rows 0 and 5 are gains near one, every other row a bias of moderate size.
All inputs are finite; a program needn't handle non-finite values.
Results may differ from a plain program's by a relative error of at most 0.011.
Values may be sent and summed in bfloat16 or wider, within the bound.
No kernel may reach another device: no remote copies, remote signals or barrier semaphores. Data moves between devices by JAX's collectives and lax.ppermute only.
A program may use at most 192 MiB of HBM per device.

v0:
```python
from functools import partial
import math

import jax
import jax.numpy as jnp
from jax import lax
from jax.experimental import pallas as pl
from jax.experimental.pallas import tpu as pltpu
from jax.sharding import PartitionSpec as P

HEAD = 64
STEP = 10

norm_eps = 1e-05
beta_one = 0.9
beta_two = 0.95
adam_eps = 1e-08
matrix_rate = 0.05
matrix_decay = 0.1
small_rate = 0.5
masked_score = -1e30
score_scale = 1.0 / math.sqrt(HEAD)

F32 = jnp.float32
BF16 = jnp.bfloat16
ALL = ("dp", "seq", "blk")
PLANE = ("seq", "blk")
VMEM_LIMIT = 56 * 1024 * 1024
NT = (((1,), (1,)), ((), ()))
TN = (((0,), (0,)), ((), ()))


def dot(a, b, dims=None):
    if dims is None:
        return jnp.dot(a, b, preferred_element_type=F32)
    return lax.dot_general(a, b, dims, preferred_element_type=F32)


def adam_update(weight, first_state, second, gradient, step_rate, decay_rate):
    moment = beta_one * first_state + (1.0 - beta_one) * gradient
    variance = beta_two * second + (1.0 - beta_two) * gradient * gradient
    mean_fixed = moment / (1.0 - beta_one**STEP)
    var_fixed = variance / (1.0 - beta_two**STEP)
    updated = weight - step_rate * (
        mean_fixed / (jnp.sqrt(var_fixed) + adam_eps) + decay_rate * weight
    )
    return (moment, variance, updated)


def norm_parts(values):
    center = jnp.mean(values, -1, keepdims=True)
    spread = values - center
    inverse = lax.rsqrt(jnp.mean(spread * spread, -1, keepdims=True) + norm_eps)
    return spread * inverse, inverse


def norm_pull(unit, inverse, gain, grad):
    scaled = grad * gain
    first = jnp.mean(scaled, -1, keepdims=True)
    second = jnp.mean(scaled * unit, -1, keepdims=True)
    return inverse * (scaled - first - unit * second)


def swap(value, seq_bits, blk_bits):
    seq_count, blk_count = lax.axis_size("seq"), lax.axis_size("blk")
    pairs = [
        (i * blk_count + j, (i ^ seq_bits) * blk_count + (j ^ blk_bits))
        for i in range(seq_count)
        for j in range(blk_count)
    ]
    return lax.ppermute(value, PLANE, pairs)


def shift(value, step):
    count = lax.axis_size("dp")
    return lax.ppermute(value, "dp", [(i, (i + step) % count) for i in range(count)])


def gather_near(value):
    return jnp.stack([value, swap(value, 0, 1), swap(value, 2, 0), swap(value, 2, 1)])


def after(value, *others):
    return lax.optimization_barrier((value, *others))[0]


def together(*values):
    return lax.optimization_barrier(values)


def gather_steps(value):
    two = jnp.stack([value, swap(value, 0, 1)])
    return jnp.concatenate([two, swap(two, 2, 0)], 0)


def add_low(a, b):
    return (a.astype(F32) + b.astype(F32)).astype(BF16)


def spread_near(both):
    return both[0], swap(both[1], 0, 1), swap(both[2], 2, 0), swap(both[3], 2, 1)


def add_all(parts):
    total = parts[0].astype(F32)
    for part in parts[1:]:
        total = total + part.astype(F32)
    return total


def spread_dp(value):
    count = lax.axis_size("dp")
    if count != 4:
        return [lax.psum_scatter(value, "dp", scatter_dimension=0, tiled=False)]
    me = lax.axis_index("dp")
    parts = [lax.dynamic_index_in_dim(value, me, 0, keepdims=False)]
    for k in range(1, count):
        chunk = lax.dynamic_index_in_dim(value, (me + k) % count, 0, keepdims=False)
        parts.append(shift(chunk, k))
    return parts


def head_masks(first, group):
    lane = lax.broadcasted_iota(jnp.int32, (1, 256), 1) - first
    return [(lane >= h * HEAD) & (lane < (h + 1) * HEAD) for h in range(group // HEAD)]


def turned(block):
    return pltpu.roll(block.astype(F32), 64, 1).astype(BF16)


def spread_heads(block, masks):
    return jnp.concatenate([jnp.where(m, block, jnp.zeros_like(block)) for m in masks], 0)


def join_heads(stacked, masks):
    rows = stacked.shape[0] // len(masks)
    out = jnp.where(masks[0], stacked[:rows], 0.0)
    for h in range(1, len(masks)):
        out = out + jnp.where(masks[h], stacked[h * rows : (h + 1) * rows], 0.0)
    return out


def visible(heads, rows, keys, first_row):
    row = lax.broadcasted_iota(jnp.int32, (heads, rows, keys), 1).reshape(heads * rows, keys)
    key = lax.broadcasted_iota(jnp.int32, (heads * rows, keys), 1)
    return key <= row + first_row


def both_rows(tok_all, at, half):
    rows = [tok_all[2 * at + half], tok_all[2 * at + 1 - half]]
    return jnp.concatenate(rows, 0).astype(F32)


def forward_kernel(pieces, place, *refs):
    me, half, layer = place[0], place[1], place[2]
    w_parts, refs = refs[: max(1, 2 * pieces)], refs[max(1, 2 * pieces) :]
    tok_all, qkv_ref, n1_ref, att_ref, lse_ref, w_ref, small_ref, w32 = refs
    rows = tok_all.shape[1]
    group = att_ref.shape[0]
    wide = w32.shape[1]
    tail = wide - 128
    w32[:, tail:wide] = jnp.zeros((w32.shape[0], 128), F32)
    if pieces == 0:
        w32[:, : w_parts[0].shape[1]] = w_parts[0][...].astype(F32)
    for k in range(pieces):
        own_layer = lax.rem(layer + (pieces - k), pieces)
        for other in range(2):
            part = w_parts[2 * k + other]
            for j in range(4):
                owner = (own_layer * 4 + (me ^ j)) * 2 + (half ^ other)
                count = part.shape[1]
                where = pl.ds(pl.multiple_of(owner * count, 8), count)
                w32[where, : part.shape[2]] = part[j].astype(F32)
    w_low = w32[...].astype(BF16)
    w_ref[...] = w_low
    first = 3 * group - tail
    small = w32[:, tail:wide].T
    small_ref[...] = small[first : first + small_ref.shape[0]]
    width = small_ref.shape[1]
    turned_small = pltpu.roll(small[first : first + 8], width - me * group, 1)
    bias = jnp.concatenate(
        [
            turned_small[2:3, :group],
            jnp.zeros((1, group), F32),
            turned_small[3:4, :group],
            jnp.zeros((1, wide - 3 * group), F32),
        ],
        1,
    )
    gain, lift = small_ref[0:1, :], small_ref[1:2, :]
    for bit in range(2):
        for far in range(2):
            at = me ^ (2 * far + bit)
            unit, _ = norm_parts(both_rows(tok_all, at, half))
            n1 = (unit * gain + lift).astype(BF16)
            out = (dot(n1, w_low) + bias).astype(BF16)
            for other in range(2):
                where = pl.ds(pl.multiple_of((2 * at + (half ^ other)) * rows, rows), rows)
                n1_ref[where, :] = n1[other * rows : (other + 1) * rows]
                qkv_ref[where, :] = out[other * rows : (other + 1) * rows]
    shifted, plain = head_masks(64, group), head_masks(0, group)
    heads = len(plain)
    for i in range(4):
        keys = 2 * rows * (i + 1)
        where = pl.ds(pl.multiple_of((2 * i + half) * rows, rows), rows)
        queries = spread_heads(turned(qkv_ref[where, 0:256]), shifted)
        scores = dot(queries, qkv_ref[0:keys, 128:384], NT) * score_scale
        seen = visible(heads, rows, keys, (2 * i + half) * rows)
        scores = jnp.where(seen, scores, masked_score)
        top = jnp.max(scores, -1, keepdims=True)
        raised = jnp.exp(scores - top)
        total = jnp.sum(raised, -1, keepdims=True)
        probs = (raised / total).astype(BF16)
        result = join_heads(dot(probs, qkv_ref[0:keys, 384:640]), plain)
        att_ref[:, i * rows : (i + 1) * rows] = result.T[:group].astype(BF16)
        lse_ref[i] = top + jnp.log(total)


def hidden_kernel(
    pieces, place, tok_all, cot_a, cot_b, att_a, att_b, vec_ref, be_ref, *refs
):
    given, refs = refs[:3], refs[3:]
    out_a, out_b, dn_a, dn_b, mixed_ref, unit_ref, inverse_ref, sums_ref, gb_ref, own_ref = refs[:10]
    g_outs, refs = refs[10:-11], refs[-11:]
    att_all, gs_sum, ge_sum, p32, proj_ref, we_ref, ws_ref, act_all, pre_all, n2_all, cot_all = refs
    me, half, layer = place[0], place[1], place[2]
    if pieces == 0:
        p32[...] = given[0][...].astype(F32)
        we_ref[...] = given[1][...]
        ws_ref[...] = given[2][...]
    else:
        p_parts, ff_ref = given[:2], given[2]
        slots, part = ws_ref.shape[0], ws_ref.shape[0] // pieces
        for k in range(pieces):
            ws_ref[k * part : (k + 1) * part, :] = ff_ref[k, 0:part, :]
            for side in range(2):
                we_ref[(2 * k + side) * part : (2 * k + side + 1) * part, :] = ff_ref[
                    k, part:, side * slots : (side + 1) * slots
                ]
        for bit in range(2):
            for j in range(4):
                for k in range(pieces):
                    own_layer = lax.rem(layer + (pieces - k), pieces)
                    owner = (own_layer * 4 + (me ^ ((j & 2) + bit))) * 2 + (half ^ (j & 1))
                    count = p_parts[bit].shape[2]
                    where = pl.ds(pl.multiple_of(owner * count, 8), count)
                    p32[where, :] = p_parts[bit][j, k].astype(F32)
    proj_ref[...] = p32[...].astype(BF16)
    rows = tok_all.shape[1]
    span = 4 * rows
    group = att_a.shape[1]
    for bit in range(2):
        att = (att_a, att_b)[bit]
        for far in range(2):
            at = me ^ (2 * far + bit)
            where = pl.ds(pl.multiple_of(at * group, 64), group)
            if bit == 0 and far == 0:
                own_ref[0:group, :] = p32[where, :].astype(BF16)
                own_ref[group:, :] = jnp.zeros((own_ref.shape[0] - group, own_ref.shape[1]), BF16)
            for other in range(2):
                att_all[where, other * span : (other + 1) * span] = att[2 * far + other]
    bias_proj, gain, lift = vec_ref[4:5, :], vec_ref[5:6, :], vec_ref[6:7, :]
    sums = [jnp.zeros((1, gain.shape[1]), F32)] * 2
    gb = jnp.zeros((1, gb_ref.shape[1]), F32)
    sums_ref[2:3, :] = jnp.sum(cot_a[0].astype(F32), 0, keepdims=True)
    for bit in range(2):
        cot, out, dn = (cot_a, cot_b)[bit], (out_a, out_b)[bit], (dn_a, dn_b)[bit]
        for far in range(2):
            start = pl.multiple_of((me ^ (2 * far + bit)) * rows, rows)
            att = jnp.concatenate(
                [
                    att_all[:, pl.ds(start, rows)],
                    att_all[:, pl.ds(pl.multiple_of(span + start, rows), rows)],
                ],
                1,
            )
            two = both_rows(tok_all, me ^ (2 * far + bit), half)
            mixed = two + (dot(att, proj_ref[...], TN) + bias_proj)
            if bit == 0 and far == 0:
                mixed_ref[...] = mixed[:rows]
            unit, inverse = norm_parts(mixed)
            if bit == 0 and far == 0:
                unit_ref[...] = unit[:rows]
                inverse_ref[...] = inverse[:rows]
            n2 = (unit * gain + lift).astype(BF16)
            pre = dot(n2, we_ref[...]) + be_ref[...]
            cots = cot[2 * far : 2 * far + 2].reshape(2 * rows, -1)
            factor = math.sqrt(2.0 / math.pi)
            square = pre * pre
            bent = jnp.tanh(factor * pre * (1.0 + 0.044715 * square))
            act = (0.5 * pre * (1.0 + bent)).astype(BF16)
            slope = 0.5 * (1.0 + bent) + 0.5 * pre * (1.0 - bent * bent) * (
                factor * (1.0 + 3.0 * 0.044715 * square)
            )
            d_act = dot(cots, ws_ref[...], NT)
            d_pre32 = d_act * slope
            d_pre = d_pre32.astype(BF16)
            d_n2 = dot(d_pre, we_ref[...], NT)
            dn[2 * far : 2 * far + 2] = d_n2.astype(BF16).reshape(2, rows, -1)
            out[2 * far : 2 * far + 2] = dot(act, ws_ref[...]).astype(BF16).reshape(2, rows, -1)
            step = pl.ds((2 * bit + far) * 2 * rows, 2 * rows)
            act_all[step, :] = act
            pre_all[step, :] = d_pre
            n2_all[step, :] = n2
            cot_all[step, :] = cots
            sums[0] = sums[0] + jnp.sum(d_n2 * unit, 0, keepdims=True)
            sums[1] = sums[1] + jnp.sum(d_n2, 0, keepdims=True)
            gb = gb + jnp.sum(d_pre.astype(F32), 0, keepdims=True)
    gs_sum[...] = dot(act_all[...], cot_all[...], TN)
    ge_sum[...] = dot(n2_all[...], pre_all[...], TN)
    sums_ref[0:1, :] = sums[0]
    sums_ref[1:2, :] = sums[1]
    gb_ref[...] = gb
    if pieces == 0:
        g_outs[0][...] = ge_sum[...].astype(BF16)
        g_outs[1][...] = gs_sum[...].astype(BF16)
        return
    pack = g_outs[0]
    for k in range(pieces):
        pack[k, 0:part, :] = gs_sum[k * part : (k + 1) * part, :].astype(BF16)
        for side in range(2):
            pack[k, part:, side * slots : (side + 1) * slots] = ge_sum[
                (2 * k + side) * part : (2 * k + side + 1) * part, :
            ].astype(BF16)


def split_halves(table, keep, send, half, row_of, lanes, at=0):
    layers, four, count, _ = keep.shape
    for k in range(layers):
        for j in range(four):
            base = row_of(k, j) * 2
            for out, owner in ((keep, base + half), (send, base + 1 - half)):
                where = pl.ds(pl.multiple_of(owner * count, 8), count)
                out[k, j, :, at : at + lanes] = table(where, j).astype(BF16)


def attention_back_kernel(
    pieces, place, db_own, db_far, db_near, db_cross, qkv_ref, lse_ref, n1_ref, own_proj, *refs
):
    d_ref, db_all, outs, (d_all, g_all) = refs[0], refs[1], refs[2:-2], refs[-2:]
    me, half = place[0], place[1]
    rows = db_own.shape[0]
    group = 3 * HEAD
    shifted, plain = head_masks(64, group), head_masks(0, group)
    heads = len(plain)
    for bits, db in ((0, db_own), (2, db_far), (1, db_near), (3, db_cross)):
        db_all[pl.ds(pl.multiple_of((me ^ bits) * rows, rows), rows), :] = db[...]
    d_all[...] = jnp.zeros_like(d_all)
    for i in range(4):
        keys = 2 * rows * (i + 1)
        where = pl.ds(pl.multiple_of((2 * i + half) * rows, rows), rows)
        queries = spread_heads(turned(qkv_ref[where, 0:256]), shifted)
        d_att = dot(db_all[i * rows : (i + 1) * rows, :], own_proj[...], NT).astype(BF16)
        grads = spread_heads(d_att, plain)
        key_rows, values = qkv_ref[0:keys, 128:384], qkv_ref[0:keys, 384:640]
        scores = dot(queries, key_rows, NT) * score_scale
        seen = visible(heads, rows, keys, (2 * i + half) * rows)
        probs = jnp.where(seen, jnp.exp(scores - lse_ref[i]), 0.0)
        weighed = probs * dot(grads, values, NT)
        d_scores = (weighed - probs * jnp.sum(weighed, -1, keepdims=True)).astype(BF16)
        dq = join_heads(dot(d_scores, key_rows), shifted) * score_scale
        d_all[where, 0:256] += pltpu.roll(dq, 192, 1)
        d_all[0:keys, 128:384] += dot(d_scores, queries, TN) * score_scale
        d_all[0:keys, 384:640] += dot(probs.astype(BF16), grads, TN)
    d_ref[...] = d_all[...].astype(BF16)
    g_all[...] = dot(n1_ref[...], d_ref[:, 0 : 2 * group], TN)
    if pieces == 0:
        outs[0][...] = g_all[...].astype(BF16)
    else:
        split_halves(
            lambda where, j: g_all[where, :], outs[0], outs[1], half, lambda k, j: k * 4 + j, 2 * group
        )


def norm_back_kernel(
    pieces, place, d_ref, db_all, n1_ref, tok_all, att_a, att_b, w_ref, two_ref, gb_ref, spot_ref,
    dn_a, dn_b, *refs
):
    outs, (g_all, gp_all) = refs[:-2], refs[-2:]
    me, half = place[0], place[1]
    rows = tok_all.shape[1]
    group = att_a.shape[1]
    wide, width = d_ref.shape[1], n1_ref.shape[1]
    sums = [jnp.zeros((1, width), F32)] * 2
    for bit in range(2):
        dn = (dn_a, dn_b)[bit]
        for far in range(2):
            at = me ^ (2 * far + bit)
            gp_all[pl.ds(pl.multiple_of(at * group, 64), group), :] = dot(
                (att_a, att_b)[bit][2 * far], db_all[...]
            )
            for other in range(2):
                where = pl.ds(pl.multiple_of((2 * at + (half ^ other)) * rows, rows), rows)
                d_n1 = dot(d_ref[where, :], w_ref[...], NT)
                unit, _ = norm_parts(tok_all[2 * at + (half ^ other)].astype(F32))
                dn[2 * far + other] = d_n1.astype(BF16)
                sums[0] = sums[0] + jnp.sum(d_n1 * unit, 0, keepdims=True)
                sums[1] = sums[1] + jnp.sum(d_n1, 0, keepdims=True)
    heads_sum = jnp.sum(d_ref[...].astype(F32), 0, keepdims=True)

    def at_heads(row):
        row = jnp.concatenate([row, jnp.zeros((1, width - group), F32)], 1)
        return pltpu.roll(jnp.broadcast_to(row, (8, width)), me * group, 1)[0:1]

    head_q, head_v = at_heads(heads_sum[:, :group]), at_heads(heads_sum[:, 2 * group : 3 * group])
    index = lax.broadcasted_iota(jnp.int32, (16, width), 0)
    small = jnp.where(index == 0, sums[0], 0.0)
    small = jnp.where(index == 1, sums[1], small)
    own = db_all[pl.ds(pl.multiple_of(me * rows, rows), rows), :].astype(F32)
    small = jnp.where(index == 4, jnp.sum(own, 0, keepdims=True), small)
    slots = gb_ref.shape[1]
    block = lax.broadcasted_iota(jnp.int32, (16, slots), 1) - 96 * (
        lax.broadcasted_iota(jnp.int32, (16, slots), 0) - 7
    )
    hidden_rows = jnp.where((block >= 0) & (block < 96), gb_ref[...], 0.0).astype(BF16)
    small = small + dot(hidden_rows, spot_ref[...])
    small = jnp.where(index == 5, two_ref[0:1, :], small)
    small = jnp.where(index == 6, two_ref[1:2, :], small)
    small = jnp.where(index == 7 + slots // 96, two_ref[2:3, :], small)
    small = jnp.where(index == 2, head_q, small)
    small = jnp.where(index == 3, head_v, small).astype(BF16)
    row = lax.broadcasted_iota(jnp.int32, (16, 256), 0)
    lane = lax.broadcasted_iota(jnp.int32, (16, 256), 1)
    spread = (lane == row + group).astype(F32).astype(BF16)
    g_all[...] = dot(n1_ref[...], d_ref[:, 2 * group :], TN) + dot(small, spread, TN)
    if pieces == 0:
        outs[0][...] = g_all[...].astype(BF16)
        outs[1][...] = gp_all[...].astype(BF16)
        return
    split_halves(
        lambda where, j: g_all[where, :], outs[0], outs[1], half, lambda k, j: k * 4 + j, 256
    )

    def chunk(where, j):
        start = j * group
        block = gp_all[where, start // 128 * 128 : start // 128 * 128 + 256]
        if start % 128:
            block = pltpu.roll(block, 256 - start % 128, 1)
        return block[:, :group]

    split_halves(chunk, outs[0], outs[1], half, lambda k, j: k * 4 + me, group, 256)


def call(kernel, outs, scratch, flops, *args):
    whole = pl.BlockSpec(memory_space=pltpu.VMEM)
    specs = [pl.BlockSpec(memory_space=pltpu.SMEM)] + [whole] * (len(args) - 1)
    moved = sum(math.prod(a.shape) * a.dtype.itemsize for a in args)
    return pl.pallas_call(
        kernel,
        out_shape=[jax.ShapeDtypeStruct(shape, kind) for shape, kind in outs],
        in_specs=specs,
        out_specs=[whole] * len(outs),
        scratch_shapes=[pltpu.VMEM(shape, kind) for shape, kind in scratch],
        compiler_params=pltpu.CompilerParams(vmem_limit_bytes=VMEM_LIMIT),
        cost_estimate=pl.CostEstimate(flops=flops, bytes_accessed=moved, transcendentals=10**6),
    )(*args)


def shards(
    tokens,
    cotangent,
    qkv_weight,
    proj_weight,
    expand_weight,
    shrink_weight,
    small_params,
    qkv_first,
    proj_first,
    expand_first,
    shrink_first,
    small_first,
    qkv_second,
    proj_second,
    expand_second,
    shrink_second,
    small_second,
):
    rows, width = tokens.shape
    hidden = expand_weight.shape[1]
    own_rows = qkv_weight.shape[0]
    own_hidden = shrink_weight.shape[0]
    dp_count, seq_count, blk_count = (lax.axis_size(a) for a in ALL)
    plane = seq_count * blk_count
    assert (seq_count, blk_count) == (4, 2)
    dp, seq, blk = (lax.axis_index(a) for a in ALL)
    spot = seq * blk_count + blk
    group = width // seq_count
    slots = hidden // plane
    length = plane * rows
    half_length = length // blk_count
    small_rows = small_params.shape[0]
    place = jnp.stack([seq, blk, dp]).astype(jnp.int32)

    w_lanes = 3 * group + small_rows
    parts = qkv_weight.astype(BF16).reshape(own_rows, 3, seq_count, group)
    parts = jnp.transpose(parts, (2, 0, 1, 3)).reshape(seq_count, own_rows, 3 * group)
    small_part = jnp.broadcast_to(
        small_params.T.astype(BF16), (seq_count, own_rows, small_rows)
    )
    parts = jnp.concatenate([parts, small_part], 2)
    pieces = 4 if dp_count == 4 and own_rows % 8 == 0 else 0
    if pieces:
        picked = [lax.dynamic_index_in_dim(parts, seq ^ k, 0, keepdims=False) for k in range(4)]
        near = jnp.stack([picked[0]] + [swap(picked[k], k, 0) for k in range(1, 4)])
        layers = [near] + [shift(near, k) for k in range(1, 4)]
        w_parts = []
        for part in layers:
            w_parts += [part, swap(part, 0, 1)]
    else:
        parts = lax.all_to_all(parts, "seq", split_axis=0, concat_axis=0, tiled=True)
        both = lax.all_gather(parts, ("dp", "blk"), axis=0, tiled=False)
        both = both.reshape(dp_count, blk_count, seq_count, own_rows, w_lanes)
        layers = [parts]
        w_parts = [jnp.transpose(both, (0, 2, 1, 3, 4)).reshape(width, w_lanes)]

    tok_all = lax.all_gather(tokens, PLANE, axis=0, tiled=False)

    expand_parts = after(expand_weight, layers[0]).astype(BF16)
    expand_parts = expand_parts.reshape(own_rows, dp_count, plane, own_hidden)
    expand_parts = jnp.transpose(expand_parts, (2, 0, 1, 3)).reshape(plane, own_rows, slots)
    expand_parts = lax.all_to_all(expand_parts, PLANE, split_axis=0, concat_axis=0, tiled=True)
    proj_low = after(proj_weight, layers[0]).astype(BF16)
    if pieces:
        proj_moved = [proj_low] + [shift(proj_low, k) for k in range(1, 4)]
    else:
        proj_moved = [proj_low]
    expand_parts = after(expand_parts, *layers, *proj_moved, w_parts[min(1, pieces)], tok_all)
    expand_parts = expand_parts.reshape(2, own_hidden, slots)
    ff_own = jnp.concatenate(
        [
            shrink_weight.astype(BF16),
            jnp.concatenate([expand_parts[0], expand_parts[1]], 1),
        ],
        0,
    )
    ff_all = lax.all_gather(ff_own, "dp", axis=0, tiled=False)

    cot_near = gather_steps(after(cotangent, layers[-1]))
    cot_a, cot_b = cot_near, swap(cot_near, 1, 0)

    if pieces:
        p_near = gather_steps(jnp.stack(proj_moved))
        hidden_weights = (p_near, swap(p_near, 1, 0), ff_all)
    else:
        w_shrink = ff_all[:, :own_hidden].reshape(slots, width)
        w_expand = jnp.stack([ff_all[:, own_hidden:, :slots], ff_all[:, own_hidden:, slots:]], 1)
        proj_whole = lax.all_gather(proj_low, ALL, axis=0, tiled=True)
        hidden_weights = (proj_whole, w_expand.reshape(width, slots), w_shrink)

    w_parts[0] = after(w_parts[0], ff_own)

    unit_at = jnp.arange(slots) % (width // plane)
    unit_at = unit_at // own_hidden * (plane * own_hidden) + spot * own_hidden + unit_at % own_hidden
    spot_table = (unit_at[:, None] == jnp.arange(width)[None]).astype(BF16)

    wide = 640
    qkv, n1, att, lse, w_qkv, small_full = call(
        partial(forward_kernel, pieces),
        [
            ((length, wide), BF16),
            ((length, width), BF16),
            ((group, half_length), BF16),
            ((4, 3 * rows, 1), F32),
            ((width, wide), BF16),
            ((small_rows, width), F32),
        ],
        [((width, wide), F32)],
        2 * 10**9,
        place, *w_parts, tok_all,
    )
    extra = hidden // width
    zero = jnp.zeros((width,), F32)
    bias_expand = small_full[7 : 7 + extra].reshape(dp_count, plane, own_hidden)
    bias_expand = lax.dynamic_index_in_dim(bias_expand, spot, 1, keepdims=False).reshape(1, slots)
    bias_shrink = small_full[7 + extra]
    att_a = after(gather_near(att), bias_expand)
    att_b = swap(att_a, 1, 0)

    big = ((4, rows, width), BF16)
    if pieces:
        hidden_grads = [((dp_count, 2 * own_hidden, width), BF16)]
    else:
        hidden_grads = [((width, slots), BF16), ((slots, width), BF16)]
    out_a, out_b, dn_a, dn_b, mixed, unit, inverse, sums_two, gb_expand, own_proj, *ff_grad = call(
        partial(hidden_kernel, pieces),
        [
            big, big, big, big,
            ((rows, width), F32),
            ((rows, width), F32),
            ((rows, 1), F32),
            ((3, width), F32),
            ((1, slots), F32),
            ((256, width), BF16),
            *hidden_grads,
        ],
        [
            ((width, length), BF16),
            ((slots, width), F32),
            ((width, slots), F32),
            ((width, width), F32),
            ((width, width), BF16),
            ((width, slots), BF16),
            ((slots, width), BF16),
            ((length, slots), BF16),
            ((length, slots), BF16),
            ((length, width), BF16),
            ((length, width), BF16),
        ],
        6 * 10**9,
        place, tok_all, cot_a, cot_b, att_a, att_b, small_full, bias_expand, *hidden_weights,
    )

    dn_both = add_low(dn_a, swap(dn_b, 1, 0))

    cot_wide = cotangent.astype(F32)
    if pieces:
        ff_grad = ff_grad[0]
    else:
        ge = ff_grad[0].reshape(dp_count, 2, own_hidden, slots)
        ff_grad = jnp.concatenate(
            [
                ff_grad[1].reshape(dp_count, own_hidden, width),
                jnp.concatenate([ge[:, 0], ge[:, 1]], 2),
            ],
            1,
        )
    ff_sum = lax.psum_scatter(
        ff_grad.reshape(-1, width), "dp", scatter_dimension=0, tiled=True
    )
    out_both = add_low(out_a, swap(after(out_b, dn_both), 1, 0))

    dn_parts = lax.optimization_barrier((*spread_near(dn_both), out_both))
    d_normed_two = add_all(dn_parts[:4])
    out_both = dn_parts[4]
    d_mixed = cot_wide + norm_pull(unit, inverse, small_full[5], d_normed_two)
    d_branch = d_mixed.astype(BF16)
    db_near = swap(d_branch, 1, 0)
    db_far = swap(d_branch, 2, 0)
    db_cross = swap(db_far, 1, 0)
    out_half = swap(after(out_both[1::2], d_branch), 0, 1)

    if pieces:
        first = ((4, 4, own_rows, 2 * group), BF16)
        second = ((4, 4, own_rows, 256 + group), BF16)
        first, second = [first] * 2, [second] * 2
    else:
        first = [((width, 2 * group), BF16)]
        second = [((width, 256), BF16), ((width, width), BF16)]
    d_low, db_all, *grads = call(
        partial(attention_back_kernel, pieces),
        [((length, wide), BF16), ((half_length, width), BF16), *first],
        [((length, wide), F32), ((width, 2 * group), F32)],
        10 * 10**9,
        place, d_branch, db_far, db_near, db_cross, qkv, lse, n1, own_proj,
    )
    grads = list(lax.optimization_barrier((*grads, out_half)))[:-1]

    def halves(table, lanes):
        table = table.reshape(dp_count, -1, blk_count, own_rows, lanes)
        keep = lax.dynamic_index_in_dim(table, blk, 2, keepdims=False)
        return keep, lax.dynamic_index_in_dim(table, 1 - blk, 2, keepdims=False)

    keep, send = grads if pieces else halves(grads[0], 2 * group)
    g_first = add_low(keep, swap(send, 0, 1))
    out_two = add_low(after(out_both, d_low)[0::2], out_half)
    out_last = swap(out_two[1], 2, 0)

    dn_a, dn_b, *grads = call(
        partial(norm_back_kernel, pieces),
        [big, big, *second],
        [((width, 256), F32), ((width, width), F32)],
        6 * 10**9,
        place, after(d_low, out_two), db_all, n1, tok_all, att_a, att_b, w_qkv,
        sums_two, gb_expand, spot_table,
    )
    if pieces:
        keep, send = grads
    else:
        v_keep, v_send = halves(grads[0], 256)
        gp = grads[1].reshape(dp_count, seq_count, blk_count, own_rows, seq_count, group)
        gp = lax.dynamic_index_in_dim(gp, seq, 1, keepdims=False)
        gp = jnp.transpose(gp, (0, 3, 1, 2, 4))
        p_keep, p_send = halves(gp, group)
        keep = jnp.concatenate([v_keep, p_keep], -1)
        send = jnp.concatenate([v_send, p_send], -1)
    g_first, keep, send, dn_a, dn_b, out_last = together(g_first, keep, send, dn_a, dn_b, out_last)
    first_parts = spread_dp(g_first)
    g_got = swap(send, 0, 1)
    dn_got = swap(dn_b, 1, 0)
    *first_parts, keep, g_got, dn_a, dn_got = together(*first_parts, keep, g_got, dn_a, dn_got)

    rest_parts = spread_dp(add_low(keep, g_got))
    dn_parts = spread_near(add_low(dn_a, dn_got))
    g_first = add_all(first_parts)
    *rest_parts, dn_0, dn_1, dn_2, dn_3 = together(*rest_parts, *dn_parts)
    g_rest = add_all(rest_parts)

    ff_sum = after(ff_sum, dn_0)
    sum_shrink = ff_sum[:own_hidden].astype(F32)
    sum_expand = ff_sum[own_hidden:]
    sum_expand = jnp.stack([sum_expand[:, :slots], sum_expand[:, slots:]])
    sum_expand = sum_expand.reshape(plane, own_rows, slots)
    sum_expand = lax.all_to_all(sum_expand, PLANE, split_axis=0, concat_axis=0, tiled=True)
    block_out = mixed + (out_two[0].astype(F32) + out_last.astype(F32)) + bias_shrink

    g_all = jnp.concatenate([g_first, g_rest[:, :, : group + small_rows]], -1).astype(BF16)
    g_all = lax.all_to_all(g_all, "seq", split_axis=0, concat_axis=0, tiled=True).astype(F32)
    sum_proj = jnp.transpose(g_rest[:, :, 256:], (1, 0, 2)).reshape(own_rows, width)
    sum_small = jnp.sum(g_all[:, :, 3 * group :], 0).T
    sum_qkv = jnp.transpose(
        g_all[:, :, : 3 * group].reshape(seq_count, own_rows, 3, group), (1, 2, 0, 3)
    ).reshape(own_rows, 3 * width)
    sum_expand = jnp.transpose(
        sum_expand.reshape(plane, own_rows, dp_count, own_hidden), (1, 2, 0, 3)
    ).reshape(own_rows, hidden).astype(F32)

    d_normed_one = add_all((dn_0, dn_1, dn_2, dn_3))
    unit, inverse = norm_parts(tokens.astype(F32))
    token_grad = d_mixed + norm_pull(unit, inverse, small_full[0], d_normed_one)

    qkv_out = adam_update(
        qkv_weight, qkv_first, qkv_second, sum_qkv, matrix_rate, matrix_decay
    )
    proj_out = adam_update(
        proj_weight, proj_first, proj_second, sum_proj, matrix_rate, matrix_decay
    )
    expand_out = adam_update(
        expand_weight, expand_first, expand_second, sum_expand, matrix_rate, matrix_decay
    )
    shrink_out = adam_update(
        shrink_weight, shrink_first, shrink_second, sum_shrink, matrix_rate, matrix_decay
    )
    small_out = adam_update(
        small_params, small_first, small_second, sum_small, small_rate, 0.0
    )
    return (block_out, token_grad, *qkv_out, *proj_out, *expand_out, *shrink_out, *small_out)


def solution(mesh):
    by_rows = P(ALL, None)
    by_columns = P(None, ALL)
    state = (by_rows,) * 4 + (by_columns,)
    return jax.shard_map(
        shards,
        mesh=mesh,
        in_specs=(by_rows, by_rows) + state * 3,
        out_specs=(by_rows,) * 14 + (by_columns,) * 3,
        check_vma=False,
    )
```

profile of v0, /device:TPU:0, one launch (start us, length us, event | category | flops | bytes accessed | tf_op | source)
XLA Modules:
  0.0 199.9 jit_solution(9204868459686942611)
XLA Ops:
  10.3 2.4 %collective-permute-start.2 = (bf16[24,588]{1,0:T(8,128)(2,1)S(1)}, bf16[24,588]{1,0:T(8,128)(2,1)S(1)}, u32[]{:S(2)}, u32[]{:S(2)}) collective-permute-start(bf16[24,588]{1,0:T(8,128)(2,1)S(1)} %get-tuple-element.215), channel_id=1, source_target_pairs={{0,6},{1,7},{2,4},{3,5},{4,2},{5,3},{6,0},{7,1},{8,14},{9,15},{10,... | collective-permute-start | bytes 84680 | tf_op jit(solution)/shard_map/ppermute | solution.py:71
  14.5 2.8 %collective-permute-done.1 = bf16[24,588]{1,0:T(8,128)(2,1)S(1)} collective-permute-done((bf16[24,588]{1,0:T(8,128)(2,1)S(1)}, bf16[24,588]{1,0:T(8,128)(2,1)S(1)}, u32[]{:S(2)}, u32[]{:S(2)}) %collective-permute-start.1) | collective-permute-done | bytes 28256 | tf_op jit(solution)/shard_map/ppermute | solution.py:71
  17.4 3.7 %collective-permute-start.3 = (bf16[4,24,588]{2,1,0:T(8,128)(2,1)S(1)}, bf16[4,24,588]{2,1,0:T(8,128)(2,1)S(1)}, u32[]{:S(2)}, u32[]{:S(2)}) collective-permute-start(bf16[4,24,588]{2,1,0:T(8,128)(2,1)S(1)} %pad_maximum_fusion.7.refs_0_), channel_id=1, source_target_pairs={{0,24},{8,0},{16,8},{24,16},{1,25},{9,1},{17,9},{25,17},{2,26},{10... | collective-permute-start | bytes 338696 | tf_op jit(solution)/shard_map/ppermute | solution.py:76
  22.2 2.9 %collective-permute-start.11 = (bf16[24,768]{1,0:T(8,128)(2,1)S(1)}, bf16[24,768]{1,0:T(8,128)(2,1)S(1)}, u32[]{:S(2)}, u32[]{:S(2)}) collective-permute-start(bf16[24,768]{1,0:T(8,128)(2,1)S(1)} %convert_element_type.165), channel_id=1, source_target_pairs={{0,24},{8,0},{16,8},{24,16},{1,25},{9,1},{17,9},{25,17},{2,26},{10... | collective-permute-start | bytes 110600 | tf_op jit(solution)/shard_map/ppermute | solution.py:76
  25.1 1.5 collective-permute-start.12
  27.7 3.4 %all-to-all-start = ((bf16[8,24,384]{2,1,0:T(8,128)(2,1)}), bf16[8,24,384]{2,1,0:T(8,128)(2,1)S(1)}, u32[]{:S(2)}, u32[]{:S(2)}) async-start(bf16[8,24,384]{2,1,0:T(8,128)(2,1)} %reshape.136), calls=%async_computation | async-start | bytes 294912 | tf_op jit(solution)/shard_map/all_to_all | solution.py:522
  31.7 1.6 collective-permute-start.8
  33.3 1.9 collective-permute-start.4
  35.3 4.0 %collective-permute-done.7.refs_2_ = bf16[4,24,588]{2,1,0:T(8,128)(2,1)S(1)} collective-permute-done((bf16[4,24,588]{2,1,0:T(8,128)(2,1)S(1)}, bf16[4,24,588]{2,1,0:T(8,128)(2,1)S(1)}, u32[]{:S(2)}, u32[]{:S(2)}) %collective-permute-start.7) | collective-permute-done | bytes 112928 | tf_op jit(solution)/shard_map/ppermute | solution.py:76
  39.3 3.9 %collective-permute-done.8.refs_4_ = bf16[4,24,588]{2,1,0:T(8,128)(2,1)S(1)} collective-permute-done((bf16[4,24,588]{2,1,0:T(8,128)(2,1)S(1)}, bf16[4,24,588]{2,1,0:T(8,128)(2,1)S(1)}, u32[]{:S(2)}, u32[]{:S(2)}) %collective-permute-start.8) | collective-permute-done | bytes 112928 | tf_op jit(solution)/shard_map/ppermute | solution.py:76
  46.0 1.6 collective-permute-start.5
  48.2 1.4 collective-permute-start.13
  50.2 1.4 collective-permute-start.15
  52.1 1.5 collective-permute-start.21
  54.7 2.6 %collective-permute-done.14.refs_5_ = bf16[4,24,588]{2,1,0:T(8,128)(2,1)S(1)} collective-permute-done((bf16[4,24,588]{2,1,0:T(8,128)(2,1)S(1)}, bf16[4,24,588]{2,1,0:T(8,128)(2,1)S(1)}, u32[]{:S(2)}, u32[]{:S(2)}) %collective-permute-start.14) | collective-permute-done | bytes 112928 | tf_op jit(solution)/shard_map/ppermute | solution.py:71
  57.3 2.0 collective-permute-done.15.refs_7_
  60.0 8.3 %shard_map.296 = (bf16[1024,640]{1,0:T(8,128)(2,1)}, bf16[1024,768]{1,0:T(8,128)(2,1)}, bf16[192,512]{1,0:T(8,128)(2,1)}, f32[4,384,1]{2,1,0:T(8,128)}, bf16[768,640]{1,0:T(8,128)(2,1)}, /*index=5*/f32[12,768]{1,0:T(8,128)}) custom-call(s32[3]{0:T(128)} %pad_add_fusion.place, bf16[4,24,588]{2,1,0:T(8,128)(2,1)} %copy-done.26, ...), custom_call_target="tpu_custom_call" | custom-call | flops 2000000000 | bytes 2476044 | tf_op jit(solution)/shard_map/pallas_call | solution.py:449
  68.8 1.3 collective-permute-start.17
  70.0 1.7 collective-permute-start.18
  73.5 1.9 collective-permute-done.16
  75.4 1.4 collective-permute-done.17
  76.8 3.4 %collective-permute-done.18 = bf16[192,512]{1,0:T(8,128)(2,1)S(1)} collective-permute-done((bf16[192,512]{1,0:T(8,128)(2,1)}, bf16[192,512]{1,0:T(8,128)(2,1)S(1)}, u32[]{:S(2)}, u32[]{:S(2)}) %collective-permute-start.18) | collective-permute-done | bytes 196640 | tf_op jit(solution)/shard_map/ppermute | solution.py:71
  80.9 1.3 pad_maximum_fusion.1.att_a
  83.0 2.5 %collective-permute-done.22.refs_1_ = bf16[4,4,24,768]{3,2,1,0:T(8,128)(2,1)S(1)} collective-permute-done((bf16[4,4,24,768]{3,2,1,0:T(8,128)(2,1)S(1)}, bf16[4,4,24,768]{3,2,1,0:T(8,128)(2,1)S(1)}, u32[]{:S(2)}, u32[]{:S(2)}) %collective-permute-start.22) | collective-permute-done | bytes 589856 | tf_op jit(solution)/shard_map/ppermute | solution.py:71
  86.3 13.5 %shard_map.297 = (bf16[4,128,768]{2,1,0:T(8,128)(2,1)}, bf16[4,128,768]{2,1,0:T(8,128)(2,1)}, bf16[4,128,768]{2,1,0:T(8,128)(2,1)}, bf16[4,128,768]{2,1,0:T(8,12...) custom-call(s32[3]{0:T(128)} %pad_add_fusion.place, ...), custom_call_target="tpu_custom_call" | custom-call | flops 6000000000 | bytes 7116300 | tf_op jit(solution)/shard_map/pallas_call | solution.py:449
  99.9 2.4 %collective-permute-done.23 = bf16[4,128,768]{2,1,0:T(8,128)(2,1)S(1)} collective-permute-done((bf16[4,128,768]{2,1,0:T(8,128)(2,1)}, bf16[4,128,768]{2,1,0:T(8,128)(2,1)S(1)}, u32[]{:S(2)}, u32[]{:S(2)}) %collective-permute-start.23) | collective-permute-done | bytes 786464 | tf_op jit(solution)/shard_map/ppermute | solution.py:71
  102.3 1.5 add_convert_fusion.2
  105.4 1.5 collective-permute-start.25
  106.9 1.7 collective-permute-start.26
  108.6 1.4 add_convert_fusion.1
  110.0 2.3 %collective-permute-done.24 = bf16[128,768]{1,0:T(8,128)(2,1)S(1)} collective-permute-done((bf16[128,768]{1,0:T(8,128)(2,1)S(1)}, bf16[128,768]{1,0:T(8,128)(2,1)S(1)}, u32[]{:S(2)}, u32[]{:S(2)}) %collective-permute-start.24) | collective-permute-done | bytes 196640 | tf_op jit(solution)/shard_map/ppermute | solution.py:71
  113.1 4.5 %collective-permute-done.26 = bf16[128,768]{1,0:T(8,128)(2,1)S(1)} collective-permute-done((bf16[128,768]{1,0:T(8,128)(2,1)S(1)}, bf16[128,768]{1,0:T(8,128)(2,1)S(1)}, u32[]{:S(2)}, u32[]{:S(2)}) %collective-permute-start.26) | collective-permute-done | bytes 196640 | tf_op jit(solution)/shard_map/ppermute | solution.py:71
  118.1 1.5 collective-permute-start.28
  119.8 4.4 %collective-permute-done.28.db_far = bf16[128,768]{1,0:T(8,128)(2,1)S(1)} collective-permute-done((bf16[128,768]{1,0:T(8,128)(2,1)S(1)}, bf16[128,768]{1,0:T(8,128)(2,1)S(1)}, u32[]{:S(2)}, u32[]{:S(2)}) %collective-permute-start.28) | collective-permute-done | bytes 196640 | tf_op jit(solution)/shard_map/ppermute | solution.py:71
  126.5 9.7 %shard_map.298 = (bf16[1024,640]{1,0:T(8,128)(2,1)}, bf16[512,768]{1,0:T(8,128)(2,1)}, bf16[4,4,24,384]{3,2,1,0:T(8,128)(2,1)}, bf16[4,4,24,384]{3,2,1,0:T(8,128)(2,1)}) custom-call(s32[3]{0:T(128)} %pad_add_fusion.place, bf16[128,768]{1,0:T(8,128)(2,1)} %copy-done.22, bf16[128,768]{1,0:T(8,128)(2,1)} %copy-done.35, bf16[128,768]{1,0:T(8,128)(2,1)} %copy-done.36, ...), custom_call_target="tpu_custom_call" | custom-call | flops 10000000000 | bytes 4069388 | tf_op jit(solution)/shard_map/pallas_call | solution.py:449
  137.0 1.5 collective-permute-start.33
  139.4 9.2 %shard_map.299 = (bf16[4,128,768]{2,1,0:T(8,128)(2,1)}, bf16[4,128,768]{2,1,0:T(8,128)(2,1)}, bf16[4,4,24,448]{3,2,1,0:T(8,128)(2,1)}, bf16[4,4,24,448]{3,2,1,0:T(8,128)(2,1)}) custom-call(s32[3]{0:T(128)} %pad_add_fusion.place, bf16[1024,640]{1,0:T(8,128)(2,1)} %get-tuple-element.114.d_ref, bf16[512,768]{1,0:T(8,128)(2,1)} %get-tuple-element.115.db_all, ...), custom_call_target="tpu_custom_call" | custom-call | flops 6000000000 | bytes 8399372 | tf_op jit(solution)/shard_map/pallas_call | solution.py:449
  150.3 2.7 %collective-permute-start.35 = (bf16[4,24,384]{2,1,0:T(8,128)(2,1)S(1)}, bf16[4,24,384]{2,1,0:T(8,128)(2,1)S(1)}, u32[]{:S(2)}, u32[]{:S(2)}) collective-permute-start(bf16[4,24,384]{2,1,0:T(8,128)(2,1)S(1)} %get-tuple-element.205), channel_id=1, source_target_pairs={{0,16},{8,24},{16,0},{24,8},{1,17},{9,25},{17,1},{25,9},{2,18},{10... | collective-permute-start | bytes 221192 | tf_op jit(solution)/shard_map/ppermute | solution.py:76
  153.1 2.8 %collective-permute-start.36 = (bf16[4,24,384]{2,1,0:T(8,128)(2,1)S(1)}, bf16[4,24,384]{2,1,0:T(8,128)(2,1)S(1)}, u32[]{:S(2)}, u32[]{:S(2)}) collective-permute-start(bf16[4,24,384]{2,1,0:T(8,128)(2,1)S(1)} %get-tuple-element.204), channel_id=1, source_target_pairs={{0,24},{8,0},{16,8},{24,16},{1,25},{9,1},{17,9},{25,17},{2,26},{10... | collective-permute-start | bytes 221192 | tf_op jit(solution)/shard_map/ppermute | solution.py:76
  156.7 2.8 %collective-permute-done.35 = bf16[4,24,384]{2,1,0:T(8,128)(2,1)S(1)} collective-permute-done((bf16[4,24,384]{2,1,0:T(8,128)(2,1)S(1)}, bf16[4,24,384]{2,1,0:T(8,128)(2,1)S(1)}, u32[]{:S(2)}, u32[]{:S(2)}) %collective-permute-start.35) | collective-permute-done | bytes 73760 | tf_op jit(solution)/shard_map/ppermute | solution.py:76
  159.5 1.3 collective-permute-done.37
  163.3 1.7 collective-permute-start.44
  165.0 2.6 %collective-permute-start.40 = (bf16[4,24,448]{2,1,0:T(8,128)(2,1)S(1)}, bf16[4,24,448]{2,1,0:T(8,128)(2,1)S(1)}, u32[]{:S(2)}, u32[]{:S(2)}) collective-permute-start(bf16[4,24,448]{2,1,0:T(8,128)(2,1)S(1)} %get-tuple-element.199), channel_id=1, source_target_pairs={{0,16},{8,24},{16,0},{24,8},{1,17},{9,25},{17,1},{25,9},{2,18},{10... | collective-permute-start | bytes 258056 | tf_op jit(solution)/shard_map/ppermute | solution.py:76
  167.6 2.9 %collective-permute-start.41 = (bf16[4,24,448]{2,1,0:T(8,128)(2,1)S(1)}, bf16[4,24,448]{2,1,0:T(8,128)(2,1)S(1)}, u32[]{:S(2)}, u32[]{:S(2)}) collective-permute-start(bf16[4,24,448]{2,1,0:T(8,128)(2,1)S(1)} %get-tuple-element.198), channel_id=1, source_target_pairs={{0,24},{8,0},{16,8},{24,16},{1,25},{9,1},{17,9},{25,17},{2,26},{10... | collective-permute-start | bytes 258056 | tf_op jit(solution)/shard_map/ppermute | solution.py:76
  170.5 3.1 %collective-permute-done.40 = bf16[4,24,448]{2,1,0:T(8,128)(2,1)S(1)} collective-permute-done((bf16[4,24,448]{2,1,0:T(8,128)(2,1)S(1)}, bf16[4,24,448]{2,1,0:T(8,128)(2,1)S(1)}, u32[]{:S(2)}, u32[]{:S(2)}) %collective-permute-start.40) | collective-permute-done | bytes 86048 | tf_op jit(solution)/shard_map/ppermute | solution.py:76
  175.4 3.3 %all-to-all-start.1 = ((bf16[4,24,588]{2,1,0:T(8,128)(2,1)}), bf16[4,24,588]{2,1,0:T(8,128)(2,1)S(1)}, u32[]{:S(2)}, u32[]{:S(2)}) async-start(bf16[4,24,588]{2,1,0:T(8,128)(2,1)} %pad_maximum_fusion.8), calls=%async_computation.1 | async-start | bytes 245760 | tf_op jit(solution)/shard_map/all_to_all | solution.py:708
  183.3 3.4 %all-to-all-start.2 = ((bf16[8,24,384]{2,1,0:T(8,128)(2,1)}), bf16[8,24,384]{2,1,0:T(8,128)(2,1)S(1)}, u32[]{:S(2)}, u32[]{:S(2)}) async-start(bf16[8,24,384]{2,1,0:T(8,128)(2,1)} %bitcast.51), calls=%async_computation.3 | async-start | bytes 294912 | tf_op jit(solution)/shard_map/all_to_all | solution.py:704
  189.1 2.5 %all-to-all-done.2 = bf16[8,24,384]{2,1,0:T(8,128)(2,1)S(1)} async-done(((bf16[8,24,384]{2,1,0:T(8,128)(2,1)}), bf16[8,24,384]{2,1,0:T(8,128)(2,1)S(1)}, u32[]{:S(2)}, u32[]{:S(2)}) %all-to-all-start.2) | async-done | bytes 147488 | tf_op jit(solution)/shard_map/all_to_all | solution.py:704
  (232 shorter events, 40.8 us)
Async XLA Ops:
  7.2 37.0 %all-gather.5.cloned.1.call-start = ((), (), s32[]{:S(2)}) async-start(), calls=%async_computation.5 | async-start | bytes 1769472 | tf_op jit(solution)/shard_map/all_gather | solution.py:517
  10.3 4.2 %collective-permute-start.2 = (bf16[24,588]{1,0:T(8,128)(2,1)S(1)}, bf16[24,588]{1,0:T(8,128)(2,1)S(1)}, u32[]{:S(2)}, u32[]{:S(2)}) collective-permute-start(bf16[24,588]{1,0:T(8,128)(2,1)S(1)} %get-tuple-element.215), channel_id=1, source_target_pairs={{0,6},{1,7},{2,4},{3,5},{4,2},{5,3},{6,0},{7,1},{8,14},{9,15},{10,... | collective-permute-start | bytes 84680 | tf_op jit(solution)/shard_map/ppermute | solution.py:71
  13.4 3.9 %collective-permute-start.1 = (bf16[24,588]{1,0:T(8,128)(2,1)S(1)}, bf16[24,588]{1,0:T(8,128)(2,1)S(1)}, u32[]{:S(2)}, u32[]{:S(2)}) collective-permute-start(bf16[24,588]{1,0:T(8,128)(2,1)S(1)} %get-tuple-element.214), channel_id=1, source_target_pairs={{0,4},{1,5},{2,6},{3,7},{4,0},{5,1},{6,2},{7,3},{8,12},{9,13},{10,... | collective-permute-start | bytes 84680 | tf_op jit(solution)/shard_map/ppermute | solution.py:71
  17.4 14.4 %collective-permute-start.3 = (bf16[4,24,588]{2,1,0:T(8,128)(2,1)S(1)}, bf16[4,24,588]{2,1,0:T(8,128)(2,1)S(1)}, u32[]{:S(2)}, u32[]{:S(2)}) collective-permute-start(bf16[4,24,588]{2,1,0:T(8,128)(2,1)S(1)} %pad_maximum_fusion.7.refs_0_), channel_id=1, source_target_pairs={{0,24},{8,0},{16,8},{24,16},{1,25},{9,1},{17,9},{25,17},{2,26},{10... | collective-permute-start | bytes 338696 | tf_op jit(solution)/shard_map/ppermute | solution.py:76
  21.0 10.1 %collective-permute-start.9 = (bf16[24,768]{1,0:T(8,128)(2,1)S(1)}, bf16[24,768]{1,0:T(8,128)(2,1)S(1)}, u32[]{:S(2)}, u32[]{:S(2)}) collective-permute-start(bf16[24,768]{1,0:T(8,128)(2,1)S(1)} %convert_element_type.165), channel_id=1, source_target_pairs={{0,8},{8,16},{16,24},{24,0},{1,9},{9,17},{17,25},{25,1},{2,10},{10... | collective-permute-start | bytes 110600 | tf_op jit(solution)/shard_map/ppermute | solution.py:76
  21.1 12.2 %collective-permute-start.10 = (bf16[24,768]{1,0:T(8,128)(2,1)S(1)}, bf16[24,768]{1,0:T(8,128)(2,1)S(1)}, u32[]{:S(2)}, u32[]{:S(2)}) collective-permute-start(bf16[24,768]{1,0:T(8,128)(2,1)S(1)} %convert_element_type.165), channel_id=1, source_target_pairs={{0,16},{8,24},{16,0},{24,8},{1,17},{9,25},{17,1},{25,9},{2,18},{10... | collective-permute-start | bytes 110600 | tf_op jit(solution)/shard_map/ppermute | solution.py:76
  22.2 13.1 %collective-permute-start.11 = (bf16[24,768]{1,0:T(8,128)(2,1)S(1)}, bf16[24,768]{1,0:T(8,128)(2,1)S(1)}, u32[]{:S(2)}, u32[]{:S(2)}) collective-permute-start(bf16[24,768]{1,0:T(8,128)(2,1)S(1)} %convert_element_type.165), channel_id=1, source_target_pairs={{0,24},{8,0},{16,8},{24,16},{1,25},{9,1},{17,9},{25,17},{2,26},{10... | collective-permute-start | bytes 110600 | tf_op jit(solution)/shard_map/ppermute | solution.py:76
  25.1 10.2 %collective-permute-start.12 = (bf16[4,24,588]{2,1,0:T(8,128)(2,1)S(1)}, bf16[4,24,588]{2,1,0:T(8,128)(2,1)S(1)}, u32[]{:S(2)}, u32[]{:S(2)}) collective-permute-start(bf16[4,24,588]{2,1,0:T(8,128)(2,1)S(1)} %pad_maximum_fusion.7.refs_0_), channel_id=1, source_target_pairs={{0,1},{1,0},{2,3},{3,2},{4,5},{5,4},{6,7},{7,6},{8,9},{9,8},{10,11... | collective-permute-start | bytes 338696 | tf_op jit(solution)/shard_map/ppermute | solution.py:71
  27.7 15.5 %all-to-all-start = ((bf16[8,24,384]{2,1,0:T(8,128)(2,1)}), bf16[8,24,384]{2,1,0:T(8,128)(2,1)S(1)}, u32[]{:S(2)}, u32[]{:S(2)}) async-start(bf16[8,24,384]{2,1,0:T(8,128)(2,1)} %reshape.136), calls=%async_computation | async-start | bytes 294912 | tf_op jit(solution)/shard_map/all_to_all | solution.py:522
  31.1 54.4 %all-gather.7.cloned.1.call-start = ((), (), s32[]{:S(2)}) async-start(), calls=%async_computation.6 | async-start | bytes 1474560 | tf_op jit(solution)/shard_map/all_gather | solution.py:537
  31.2 8.1 %collective-permute-start.7 = (bf16[4,24,588]{2,1,0:T(8,128)(2,1)S(1)}, bf16[4,24,588]{2,1,0:T(8,128)(2,1)S(1)}, u32[]{:S(2)}, u32[]{:S(2)}) collective-permute-start(bf16[4,24,588]{2,1,0:T(8,128)(2,1)S(1)} %pad_maximum_fusion.7.refs_0_), channel_id=1, source_target_pairs={{0,8},{8,16},{16,24},{24,0},{1,9},{9,17},{17,25},{25,1},{2,10},{10... | collective-permute-start | bytes 338696 | tf_op jit(solution)/shard_map/ppermute | solution.py:76
  31.7 11.5 %collective-permute-start.8 = (bf16[4,24,588]{2,1,0:T(8,128)(2,1)S(1)}, bf16[4,24,588]{2,1,0:T(8,128)(2,1)S(1)}, u32[]{:S(2)}, u32[]{:S(2)}) collective-permute-start(bf16[4,24,588]{2,1,0:T(8,128)(2,1)S(1)} %pad_maximum_fusion.7.refs_0_), channel_id=1, source_target_pairs={{0,16},{8,24},{16,0},{24,8},{1,17},{9,25},{17,1},{25,9},{2,18},{10... | collective-permute-start | bytes 338696 | tf_op jit(solution)/shard_map/ppermute | solution.py:76
  33.3 12.7 %collective-permute-start.4 = (bf16[128,768]{1,0:T(8,128)(2,1)S(1)}, bf16[128,768]{1,0:T(8,128)(2,1)S(1)}, u32[]{:S(2)}, u32[]{:S(2)}) collective-permute-start(bf16[128,768]{1,0:T(8,128)(2,1)S(1)} %copy-done.1), channel_id=1, source_target_pairs={{0,1},{1,0},{2,3},{3,2},{4,5},{5,4},{6,7},{7,6},{8,9},{9,8},{10,11... | collective-permute-start | bytes 589832 | tf_op jit(solution)/shard_map/ppermute | solution.py:71
  45.1 128.7 %reduce-scatter.2.cloned.1.call-start = ((), (), s32[]{:S(2)}) async-start(), calls=%async_computation.4 | async-start | bytes 1474560 | tf_op jit(solution)/shard_map/reduce_scatter | solution.py:628
  45.3 6.7 %collective-permute-start.20 = (bf16[4,24,768]{2,1,0:T(8,128)(2,1)S(1)}, bf16[4,24,768]{2,1,0:T(8,128)(2,1)S(1)}, u32[]{:S(2)}, u32[]{:S(2)}) collective-permute-start(bf16[4,24,768]{2,1,0:T(8,128)(2,1)S(1)} %get-tuple-element.209), channel_id=1, source_target_pairs={{0,1},{1,0},{2,3},{3,2},{4,5},{5,4},{6,7},{7,6},{8,9},{9,8},{10,11... | collective-permute-start | bytes 442376 | tf_op jit(solution)/shard_map/ppermute | solution.py:71
  46.0 25.7 %collective-permute-start.5 = (bf16[2,128,768]{2,1,0:T(8,128)(2,1)S(1)}, bf16[2,128,768]{2,1,0:T(8,128)(2,1)S(1)}, u32[]{:S(2)}, u32[]{:S(2)}) collective-permute-start(bf16[2,128,768]{2,1,0:T(8,128)(2,1)S(1)} %pad_maximum_fusion.3), channel_id=1, source_target_pairs={{0,4},{1,5},{2,6},{3,7},{4,0},{5,1},{6,2},{7,3},{8,12},{9,13},{10,... | collective-permute-start | bytes 1179656 | tf_op jit(solution)/shard_map/ppermute | solution.py:71
  48.2 6.5 %collective-permute-start.13 = (bf16[4,24,588]{2,1,0:T(8,128)(2,1)S(1)}, bf16[4,24,588]{2,1,0:T(8,128)(2,1)S(1)}, u32[]{:S(2)}, u32[]{:S(2)}) collective-permute-start(bf16[4,24,588]{2,1,0:T(8,128)(2,1)S(1)} %collective-permute-done.7.refs_2_), channel_id=1, source_target_pairs={{0,1},{1,0},{2,3},{3,2},{4,5},{5,4},{6,7},{7,6},{8,9},{9,8},{10,11... | collective-permute-start | bytes 338696 | tf_op jit(solution)/shard_map/ppermute | solution.py:71
  49.6 7.7 %collective-permute-start.14 = (bf16[4,24,588]{2,1,0:T(8,128)(2,1)S(1)}, bf16[4,24,588]{2,1,0:T(8,128)(2,1)S(1)}, u32[]{:S(2)}, u32[]{:S(2)}) collective-permute-start(bf16[4,24,588]{2,1,0:T(8,128)(2,1)S(1)} %collective-permute-done.8.refs_4_), channel_id=1, source_target_pairs={{0,1},{1,0},{2,3},{3,2},{4,5},{5,4},{6,7},{7,6},{8,9},{9,8},{10,11... | collective-permute-start | bytes 338696 | tf_op jit(solution)/shard_map/ppermute | solution.py:71
  50.2 9.1 %collective-permute-start.15 = (bf16[4,24,588]{2,1,0:T(8,128)(2,1)S(1)}, bf16[4,24,588]{2,1,0:T(8,128)(2,1)S(1)}, u32[]{:S(2)}, u32[]{:S(2)}) collective-permute-start(bf16[4,24,588]{2,1,0:T(8,128)(2,1)S(1)} %collective-permute-done.3.refs_6_), channel_id=1, source_target_pairs={{0,1},{1,0},{2,3},{3,2},{4,5},{5,4},{6,7},{7,6},{8,9},{9,8},{10,11... | collective-permute-start | bytes 338696 | tf_op jit(solution)/shard_map/ppermute | solution.py:71
  52.1 30.2 %collective-permute-start.21 = (bf16[2,4,24,768]{3,2,1,0:T(8,128)(2,1)S(1)}, bf16[2,4,24,768]{3,2,1,0:T(8,128)(2,1)S(1)}, u32[]{:S(2)}, u32[]{:S(2)}) collective-permute-start(bf16[2,4,24,768]{3,2,1,0:T(8,128)(2,1)S(1)} %pad_maximum_fusion.4), channel_id=1, source_target_pairs={{0,4},{1,5},{2,6},{3,7},{4,0},{5,1},{6,2},{7,3},{8,12},{9,13},{10,... | collective-permute-start | bytes 884744 | tf_op jit(solution)/shard_map/ppermute | solution.py:71
  68.3 7.1 %collective-permute-start.16 = (bf16[192,512]{1,0:T(8,128)(2,1)}, bf16[192,512]{1,0:T(8,128)(2,1)S(1)}, u32[]{:S(2)}, u32[]{:S(2)}) collective-permute-start(bf16[192,512]{1,0:T(8,128)(2,1)} %get-tuple-element.87), channel_id=1, source_target_pairs={{0,1},{1,0},{2,3},{3,2},{4,5},{5,4},{6,7},{7,6},{8,9},{9,8},{10,11... | collective-permute-start | bytes 589832 | tf_op jit(solution)/shard_map/ppermute | solution.py:71
  68.8 8.1 %collective-permute-start.17 = (bf16[192,512]{1,0:T(8,128)(2,1)}, bf16[192,512]{1,0:T(8,128)(2,1)S(1)}, u32[]{:S(2)}, u32[]{:S(2)}) collective-permute-start(bf16[192,512]{1,0:T(8,128)(2,1)} %get-tuple-element.87), channel_id=1, source_target_pairs={{0,4},{1,5},{2,6},{3,7},{4,0},{5,1},{6,2},{7,3},{8,12},{9,13},{10,... | collective-permute-start | bytes 589832 | tf_op jit(solution)/shard_map/ppermute | solution.py:71
  70.0 10.2 %collective-permute-start.18 = (bf16[192,512]{1,0:T(8,128)(2,1)}, bf16[192,512]{1,0:T(8,128)(2,1)S(1)}, u32[]{:S(2)}, u32[]{:S(2)}) collective-permute-start(bf16[192,512]{1,0:T(8,128)(2,1)} %get-tuple-element.87), channel_id=1, source_target_pairs={{0,5},{1,4},{2,7},{3,6},{4,1},{5,0},{6,3},{7,2},{8,13},{9,12},{10,... | collective-permute-start | bytes 589832 | tf_op jit(solution)/shard_map/ppermute | solution.py:71
  71.8 13.6 %collective-permute-start.6 = (bf16[4,128,768]{2,1,0:T(8,128)(2,1)S(1)}, bf16[4,128,768]{2,1,0:T(8,128)(2,1)}, u32[]{:S(2)}, u32[]{:S(2)}) collective-permute-start(bf16[4,128,768]{2,1,0:T(8,128)(2,1)S(1)} %pad_maximum_fusion.cot_a), channel_id=1, source_target_pairs={{0,2},{1,3},{2,0},{3,1},{4,6},{5,7},{6,4},{7,5},{8,10},{9,11},{10,... | collective-permute-start | bytes 2359304 | tf_op jit(solution)/shard_map/ppermute | solution.py:71
  82.3 3.2 %collective-permute-start.19 = (bf16[4,192,512]{2,1,0:T(8,128)(2,1)S(1)}, bf16[4,192,512]{2,1,0:T(8,128)(2,1)}, u32[]{:S(2)}, u32[]{:S(2)}) collective-permute-start(bf16[4,192,512]{2,1,0:T(8,128)(2,1)S(1)} %pad_maximum_fusion.1.att_a), channel_id=1, source_target_pairs={{0,2},{1,3},{2,0},{3,1},{4,6},{5,7},{6,4},{7,5},{8,10},{9,11},{10,... | collective-permute-start | bytes 2359304 | tf_op jit(solution)/shard_map/ppermute | solution.py:71
  82.4 3.0 %collective-permute-start.22 = (bf16[4,4,24,768]{3,2,1,0:T(8,128)(2,1)S(1)}, bf16[4,4,24,768]{3,2,1,0:T(8,128)(2,1)S(1)}, u32[]{:S(2)}, u32[]{:S(2)}) collective-permute-start(bf16[4,4,24,768]{3,2,1,0:T(8,128)(2,1)S(1)} %pad_maximum_fusion.2.refs_0_), channel_id=1, source_target_pairs={{0,2},{1,3},{2,0},{3,1},{4,6},{5,7},{6,4},{7,5},{8,10},{9,11},{10,... | collective-permute-start | bytes 1769480 | tf_op jit(solution)/shard_map/ppermute | solution.py:71
  103.8 4.8 %collective-permute-start.27 = (bf16[4,128,768]{2,1,0:T(8,128)(2,1)}, bf16[4,128,768]{2,1,0:T(8,128)(2,1)}, u32[]{:S(2)}, u32[]{:S(2)}) collective-permute-start(bf16[4,128,768]{2,1,0:T(8,128)(2,1)} %get-tuple-element.95), channel_id=1, source_target_pairs={{0,2},{1,3},{2,0},{3,1},{4,6},{5,7},{6,4},{7,5},{8,10},{9,11},{10,... | collective-permute-start | bytes 2359304 | tf_op jit(solution)/shard_map/ppermute | solution.py:71
  105.0 7.2 %collective-permute-start.24 = (bf16[128,768]{1,0:T(8,128)(2,1)S(1)}, bf16[128,768]{1,0:T(8,128)(2,1)S(1)}, u32[]{:S(2)}, u32[]{:S(2)}) collective-permute-start(bf16[128,768]{1,0:T(8,128)(2,1)S(1)} %get-tuple-element.196), channel_id=1, source_target_pairs={{0,1},{1,0},{2,3},{3,2},{4,5},{5,4},{6,7},{7,6},{8,9},{9,8},{10,11... | collective-permute-start | bytes 589832 | tf_op jit(solution)/shard_map/ppermute | solution.py:71
  105.4 7.7 %collective-permute-start.25 = (bf16[128,768]{1,0:T(8,128)(2,1)S(1)}, bf16[128,768]{1,0:T(8,128)(2,1)S(1)}, u32[]{:S(2)}, u32[]{:S(2)}) collective-permute-start(bf16[128,768]{1,0:T(8,128)(2,1)S(1)} %get-tuple-element.195), channel_id=1, source_target_pairs={{0,4},{1,5},{2,6},{3,7},{4,0},{5,1},{6,2},{7,3},{8,12},{9,13},{10,... | collective-permute-start | bytes 589832 | tf_op jit(solution)/shard_map/ppermute | solution.py:71
  106.9 10.8 %collective-permute-start.26 = (bf16[128,768]{1,0:T(8,128)(2,1)S(1)}, bf16[128,768]{1,0:T(8,128)(2,1)S(1)}, u32[]{:S(2)}, u32[]{:S(2)}) collective-permute-start(bf16[128,768]{1,0:T(8,128)(2,1)S(1)} %get-tuple-element.194), channel_id=1, source_target_pairs={{0,5},{1,4},{2,7},{3,6},{4,1},{5,0},{6,3},{7,2},{8,13},{9,12},{10,... | collective-permute-start | bytes 589832 | tf_op jit(solution)/shard_map/ppermute | solution.py:71
  118.1 6.1 %collective-permute-start.28 = (bf16[128,768]{1,0:T(8,128)(2,1)S(1)}, bf16[128,768]{1,0:T(8,128)(2,1)S(1)}, u32[]{:S(2)}, u32[]{:S(2)}) collective-permute-start(bf16[128,768]{1,0:T(8,128)(2,1)S(1)} %get-tuple-element.187.db_own), channel_id=1, source_target_pairs={{0,4},{1,5},{2,6},{3,7},{4,0},{5,1},{6,2},{7,3},{8,12},{9,13},{10,... | collective-permute-start | bytes 589832 | tf_op jit(solution)/shard_map/ppermute | solution.py:71
  119.7 6.0 %collective-permute-start.29 = (bf16[128,768]{1,0:T(8,128)(2,1)S(1)}, bf16[128,768]{1,0:T(8,128)(2,1)S(1)}, u32[]{:S(2)}, u32[]{:S(2)}) collective-permute-start(bf16[128,768]{1,0:T(8,128)(2,1)S(1)} %get-tuple-element.187.db_own), channel_id=1, source_target_pairs={{0,2},{1,3},{2,0},{3,1},{4,6},{5,7},{6,4},{7,5},{8,10},{9,11},{10,... | collective-permute-start | bytes 589832 | tf_op jit(solution)/shard_map/ppermute | solution.py:71
  125.2 11.6 %collective-permute-start.31 = (bf16[2,128,768]{2,1,0:T(8,128)(2,1)S(1)}, bf16[2,128,768]{2,1,0:T(8,128)(2,1)S(1)}, u32[]{:S(2)}, u32[]{:S(2)}) collective-permute-start(bf16[2,128,768]{2,1,0:T(8,128)(2,1)S(1)} %slice.90), channel_id=1, source_target_pairs={{0,1},{1,0},{2,3},{3,2},{4,5},{5,4},{6,7},{7,6},{8,9},{9,8},{10,11... | collective-permute-start | bytes 1179656 | tf_op jit(solution)/shard_map/ppermute | solution.py:71
  137.0 11.8 %collective-permute-start.33 = (bf16[128,768]{1,0:T(8,128)(2,1)S(1)}, bf16[128,768]{1,0:T(8,128)(2,1)S(1)}, u32[]{:S(2)}, u32[]{:S(2)}) collective-permute-start(bf16[128,768]{1,0:T(8,128)(2,1)S(1)} %slice_bitcast_fusion.4), channel_id=1, source_target_pairs={{0,4},{1,5},{2,6},{3,7},{4,0},{5,1},{6,2},{7,3},{8,12},{9,13},{10,... | collective-permute-start | bytes 589832 | tf_op jit(solution)/shard_map/ppermute | solution.py:71
  138.4 10.2 %collective-permute-start.32 = (bf16[4,4,24,384]{3,2,1,0:T(8,128)(2,1)S(1)}, bf16[4,4,24,384]{3,2,1,0:T(8,128)(2,1)S(1)}, u32[]{:S(2)}, u32[]{:S(2)}) collective-permute-start(bf16[4,4,24,384]{3,2,1,0:T(8,128)(2,1)S(1)} %copy-done.34), channel_id=1, source_target_pairs={{0,1},{1,0},{2,3},{3,2},{4,5},{5,4},{6,7},{7,6},{8,9},{9,8},{10,11... | collective-permute-start | bytes 884744 | tf_op jit(solution)/shard_map/ppermute | solution.py:71
  148.7 12.1 %collective-permute-start.38 = (bf16[4,128,768]{2,1,0:T(8,128)(2,1)}, bf16[4,128,768]{2,1,0:T(8,128)(2,1)S(1)}, u32[]{:S(2)}, u32[]{:S(2)}) collective-permute-start(bf16[4,128,768]{2,1,0:T(8,128)(2,1)} %get-tuple-element.128), channel_id=1, source_target_pairs={{0,2},{1,3},{2,0},{3,1},{4,6},{5,7},{6,4},{7,5},{8,10},{9,11},{10,... | collective-permute-start | bytes 2359304 | tf_op jit(solution)/shard_map/ppermute | solution.py:71
  149.1 11.7 %collective-permute-start.37 = (bf16[4,4,24,448]{3,2,1,0:T(8,128)(2,1)}, bf16[4,4,24,448]{3,2,1,0:T(8,128)(2,1)S(1)}, u32[]{:S(2)}, u32[]{:S(2)}) collective-permute-start(bf16[4,4,24,448]{3,2,1,0:T(8,128)(2,1)} %get-tuple-element.126), channel_id=1, source_target_pairs={{0,1},{1,0},{2,3},{3,2},{4,5},{5,4},{6,7},{7,6},{8,9},{9,8},{10,11... | collective-permute-start | bytes 1032200 | tf_op jit(solution)/shard_map/ppermute | solution.py:71
  150.3 6.5 %collective-permute-start.34 = (bf16[4,24,384]{2,1,0:T(8,128)(2,1)S(1)}, bf16[4,24,384]{2,1,0:T(8,128)(2,1)S(1)}, u32[]{:S(2)}, u32[]{:S(2)}) collective-permute-start(bf16[4,24,384]{2,1,0:T(8,128)(2,1)S(1)} %get-tuple-element.206), channel_id=1, source_target_pairs={{0,8},{8,16},{16,24},{24,0},{1,9},{9,17},{17,25},{25,1},{2,10},{10... | collective-permute-start | bytes 221192 | tf_op jit(solution)/shard_map/ppermute | solution.py:76
  150.3 9.2 %collective-permute-start.35 = (bf16[4,24,384]{2,1,0:T(8,128)(2,1)S(1)}, bf16[4,24,384]{2,1,0:T(8,128)(2,1)S(1)}, u32[]{:S(2)}, u32[]{:S(2)}) collective-permute-start(bf16[4,24,384]{2,1,0:T(8,128)(2,1)S(1)} %get-tuple-element.205), channel_id=1, source_target_pairs={{0,16},{8,24},{16,0},{24,8},{1,17},{9,25},{17,1},{25,9},{2,18},{10... | collective-permute-start | bytes 221192 | tf_op jit(solution)/shard_map/ppermute | solution.py:76
  153.1 6.4 %collective-permute-start.36 = (bf16[4,24,384]{2,1,0:T(8,128)(2,1)S(1)}, bf16[4,24,384]{2,1,0:T(8,128)(2,1)S(1)}, u32[]{:S(2)}, u32[]{:S(2)}) collective-permute-start(bf16[4,24,384]{2,1,0:T(8,128)(2,1)S(1)} %get-tuple-element.204), channel_id=1, source_target_pairs={{0,24},{8,0},{16,8},{24,16},{1,25},{9,1},{17,9},{25,17},{2,26},{10... | collective-permute-start | bytes 221192 | tf_op jit(solution)/shard_map/ppermute | solution.py:76
  161.0 6.6 %collective-permute-start.39 = (bf16[4,24,448]{2,1,0:T(8,128)(2,1)S(1)}, bf16[4,24,448]{2,1,0:T(8,128)(2,1)S(1)}, u32[]{:S(2)}, u32[]{:S(2)}) collective-permute-start(bf16[4,24,448]{2,1,0:T(8,128)(2,1)S(1)} %get-tuple-element.200), channel_id=1, source_target_pairs={{0,8},{8,16},{16,24},{24,0},{1,9},{9,17},{17,25},{25,1},{2,10},{10... | collective-permute-start | bytes 258056 | tf_op jit(solution)/shard_map/ppermute | solution.py:76
  161.5 12.2 %collective-permute-start.42 = (bf16[128,768]{1,0:T(8,128)(2,1)S(1)}, bf16[128,768]{1,0:T(8,128)(2,1)S(1)}, u32[]{:S(2)}, u32[]{:S(2)}) collective-permute-start(bf16[128,768]{1,0:T(8,128)(2,1)S(1)} %get-tuple-element.192), channel_id=1, source_target_pairs={{0,1},{1,0},{2,3},{3,2},{4,5},{5,4},{6,7},{7,6},{8,9},{9,8},{10,11... | collective-permute-start | bytes 589832 | tf_op jit(solution)/shard_map/ppermute | solution.py:71
  162.5 11.1 %collective-permute-start.43 = (bf16[128,768]{1,0:T(8,128)(2,1)S(1)}, bf16[128,768]{1,0:T(8,128)(2,1)S(1)}, u32[]{:S(2)}, u32[]{:S(2)}) collective-permute-start(bf16[128,768]{1,0:T(8,128)(2,1)S(1)} %get-tuple-element.191), channel_id=1, source_target_pairs={{0,4},{1,5},{2,6},{3,7},{4,0},{5,1},{6,2},{7,3},{8,12},{9,13},{10,... | collective-permute-start | bytes 589832 | tf_op jit(solution)/shard_map/ppermute | solution.py:71
  163.3 10.3 %collective-permute-start.44 = (bf16[128,768]{1,0:T(8,128)(2,1)S(1)}, bf16[128,768]{1,0:T(8,128)(2,1)S(1)}, u32[]{:S(2)}, u32[]{:S(2)}) collective-permute-start(bf16[128,768]{1,0:T(8,128)(2,1)S(1)} %get-tuple-element.190), channel_id=1, source_target_pairs={{0,5},{1,4},{2,7},{3,6},{4,1},{5,0},{6,3},{7,2},{8,13},{9,12},{10,... | collective-permute-start | bytes 589832 | tf_op jit(solution)/shard_map/ppermute | solution.py:71
  165.0 8.6 %collective-permute-start.40 = (bf16[4,24,448]{2,1,0:T(8,128)(2,1)S(1)}, bf16[4,24,448]{2,1,0:T(8,128)(2,1)S(1)}, u32[]{:S(2)}, u32[]{:S(2)}) collective-permute-start(bf16[4,24,448]{2,1,0:T(8,128)(2,1)S(1)} %get-tuple-element.199), channel_id=1, source_target_pairs={{0,16},{8,24},{16,0},{24,8},{1,17},{9,25},{17,1},{25,9},{2,18},{10... | collective-permute-start | bytes 258056 | tf_op jit(solution)/shard_map/ppermute | solution.py:76
  167.6 6.0 %collective-permute-start.41 = (bf16[4,24,448]{2,1,0:T(8,128)(2,1)S(1)}, bf16[4,24,448]{2,1,0:T(8,128)(2,1)S(1)}, u32[]{:S(2)}, u32[]{:S(2)}) collective-permute-start(bf16[4,24,448]{2,1,0:T(8,128)(2,1)S(1)} %get-tuple-element.198), channel_id=1, source_target_pairs={{0,24},{8,0},{16,8},{24,16},{1,25},{9,1},{17,9},{25,17},{2,26},{10... | collective-permute-start | bytes 258056 | tf_op jit(solution)/shard_map/ppermute | solution.py:76
  175.4 7.8 %all-to-all-start.1 = ((bf16[4,24,588]{2,1,0:T(8,128)(2,1)}), bf16[4,24,588]{2,1,0:T(8,128)(2,1)S(1)}, u32[]{:S(2)}, u32[]{:S(2)}) async-start(bf16[4,24,588]{2,1,0:T(8,128)(2,1)} %pad_maximum_fusion.8), calls=%async_computation.1 | async-start | bytes 245760 | tf_op jit(solution)/shard_map/all_to_all | solution.py:708
  183.3 8.3 %all-to-all-start.2 = ((bf16[8,24,384]{2,1,0:T(8,128)(2,1)}), bf16[8,24,384]{2,1,0:T(8,128)(2,1)S(1)}, u32[]{:S(2)}, u32[]{:S(2)}) async-start(bf16[8,24,384]{2,1,0:T(8,128)(2,1)} %bitcast.51), calls=%async_computation.3 | async-start | bytes 294912 | tf_op jit(solution)/shard_map/all_to_all | solution.py:704
  (48 other events, 343.3 us)
Sparse Core Ops, SparseCore 0:
  9.9 34.2 all-gather.4
  46.4 29.7 all-gather.6
  125.3 28.6 reduce-scatter.1
where the time goes:
time: 201 us; the launch traced here: 200 us
  starting transfers between devices  62.6 us (31%)
  waiting for transfers between devices  54.4 us (27%)
  Pallas kernels  40.6 us (20%)
  other arithmetic  17.8 us (9%)
  between operations  14.7 us (7%)
  local copies, waits for them, and re-layouts  9.77 us (5%)
    pallas_call x4, Pallas kernels, call(): pl.pallas_call(kernel, out_shape=[jax.ShapeDtypeStruct(shape, kind) for s...  40.6 us
    ppermute x33, waiting for transfers between devices, swap(): return lax.ppermute(value, PLANE, pairs)  35.7 us
    ppermute x33, starting transfers between devices, swap(): return lax.ppermute(value, PLANE, pairs)  31.1 us
    ppermute x12, starting transfers between devices, shift(): lax.ppermute(value, 'dp', [(i, (i + step) % count) for i in range(count)])  21.1 us
    ppermute x12, waiting for transfers between devices, shift(): lax.ppermute(value, 'dp', [(i, (i + step) % count) for i in range(count)])  13.8 us
    sub x5, other arithmetic, adam_update(): weight - step_rate * (mean_fixed / (jnp.sqrt(var_fixed) + adam_eps) + dec...  4.36 us
  transfers between devices with their start and end apart: 51, of which 24 were waited for; matrix products, arithmetic and copies ran while one was open for 10% of the time, Pallas kernels for 14%

commit v1 on v0

--- a/solution.py
+++ b/solution.py
@@ -520,7 +520,7 @@
     expand_parts = expand_parts.reshape(own_rows, dp_count, plane, own_hidden)
     expand_parts = jnp.transpose(expand_parts, (2, 0, 1, 3)).reshape(plane, own_rows, slots)
     expand_parts = lax.all_to_all(expand_parts, PLANE, split_axis=0, concat_axis=0, tiled=True)
-    proj_low = after(proj_weight, layers[0]).astype(BF16)
+    proj_low = after(proj_weight, expand_parts).astype(BF16)
     if pieces:
         proj_moved = [proj_low] + [shift(proj_low, k) for k in range(1, 4)]
     else:
@@ -536,11 +536,13 @@
     )
     ff_all = lax.all_gather(ff_own, "dp", axis=0, tiled=False)
 
-    cot_near = gather_steps(after(cotangent, layers[-1]))
-    cot_a, cot_b = cot_near, swap(cot_near, 1, 0)
+    gate = w_parts[3 * (pieces > 0)]
+    cot_low = after(cotangent, layers[-1])
+    cot_two = after(jnp.stack([cot_low, swap(cot_low, 0, 1)]), gate)
+    cot_far = swap(cot_two, 2, 0)
 
     if pieces:
-        p_near = gather_steps(jnp.stack(proj_moved))
+        p_near = gather_steps(after(jnp.stack(proj_moved), gate))
         hidden_weights = (p_near, swap(p_near, 1, 0), ff_all)
     else:
         w_shrink = ff_all[:, :own_hidden].reshape(slots, width)
@@ -574,7 +576,13 @@
     bias_expand = small_full[7 : 7 + extra].reshape(dp_count, plane, own_hidden)
     bias_expand = lax.dynamic_index_in_dim(bias_expand, spot, 1, keepdims=False).reshape(1, slots)
     bias_shrink = small_full[7 + extra]
-    att_a = after(gather_near(att), bias_expand)
+    att, cot_two, cot_far = together(att, cot_two, cot_far)
+    cot_a = jnp.concatenate([cot_two, cot_far], 0)
+    cot_b = swap(cot_a, 1, 0)
+    gain_one, gain_two = small_full[0], small_full[5]
+    att_a, bias_expand, bias_shrink, gain_one, gain_two, spot_table = together(
+        gather_near(att), bias_expand, bias_shrink, gain_one, gain_two, spot_table
+    )
     att_b = swap(att_a, 1, 0)
 
     big = ((4, rows, width), BF16)
@@ -633,7 +641,7 @@
     dn_parts = lax.optimization_barrier((*spread_near(dn_both), out_both))
     d_normed_two = add_all(dn_parts[:4])
     out_both = dn_parts[4]
-    d_mixed = cot_wide + norm_pull(unit, inverse, small_full[5], d_normed_two)
+    d_mixed = cot_wide + norm_pull(unit, inverse, gain_two, d_normed_two)
     d_branch = d_mixed.astype(BF16)
     db_near = swap(d_branch, 1, 0)
     db_far = swap(d_branch, 2, 0)
@@ -705,9 +713,12 @@
     block_out = mixed + (out_two[0].astype(F32) + out_last.astype(F32)) + bias_shrink
 
     g_all = jnp.concatenate([g_first, g_rest[:, :, : group + small_rows]], -1).astype(BF16)
-    g_all = lax.all_to_all(g_all, "seq", split_axis=0, concat_axis=0, tiled=True).astype(F32)
+    picked = [lax.dynamic_index_in_dim(g_all, seq ^ k, 0, keepdims=False) for k in range(4)]
+    picked = jnp.stack([picked[0]] + [swap(picked[k], k, 0) for k in range(1, 4)]).astype(F32)
+    g_all = [lax.dynamic_index_in_dim(picked, seq ^ k, 0, keepdims=False) for k in range(4)]
+    g_all = jnp.stack(g_all)
     sum_proj = jnp.transpose(g_rest[:, :, 256:], (1, 0, 2)).reshape(own_rows, width)
-    sum_small = jnp.sum(g_all[:, :, 3 * group :], 0).T
+    sum_small = jnp.sum(picked[:, :, 3 * group :], 0).T
     sum_qkv = jnp.transpose(
         g_all[:, :, : 3 * group].reshape(seq_count, own_rows, 3, group), (1, 2, 0, 3)
     ).reshape(own_rows, 3 * width)
@@ -717,7 +728,7 @@
 
     d_normed_one = add_all((dn_0, dn_1, dn_2, dn_3))
     unit, inverse = norm_parts(tokens.astype(F32))
-    token_grad = d_mixed + norm_pull(unit, inverse, small_full[0], d_normed_one)
+    token_grad = d_mixed + norm_pull(unit, inverse, gain_one, d_normed_one)
 
     qkv_out = adam_update(
         qkv_weight, qkv_first, qkv_second, sum_qkv, matrix_rate, matrix_decay

time: 201 us -> 190 us (0.945)
  waiting for transfers between devices: 54.4 us -> 46.2 us
  starting transfers between devices: 62.6 us -> 59.5 us
    ppermute x12, waiting for transfers between devices: 13.8 us -> 8.96 us  [shift(): lax.ppermute(value, 'dp', [(i, (i + step) % count) for i in range(count)])]
    all_to_all x1 -> x0, starting transfers between devices: 3.32 us -> none  [shards(): lax.all_to_all(g_all, 'seq', split_axis=0, concat_axis=0, tiled=True)]
    all_to_all x1, waiting for transfers between devices: 2.48 us -> 0.01 us  [shards(): lax.all_to_all(sum_expand, PLANE, split_axis=0, concat_axis=0, tiled=True)]
    ppermute x33 -> x36, starting transfers between devices: 31.1 us -> 33.3 us  [swap(): return lax.ppermute(value, PLANE, pairs)]
    ppermute x33 -> x36, waiting for transfers between devices: 35.7 us -> 34.6 us  [swap(): return lax.ppermute(value, PLANE, pairs)]
  transfers between devices with their start and end apart: 51 -> 53, of which waited for: 24 -> 24; matrix products, arithmetic and copies ran while one was open for 10% -> 10% of each run, Pallas kernels for 14% -> 14%
where the time goes in v1:
time: 190 us; the launch traced here: 189 us
  starting transfers between devices  59.5 us (31%)
  waiting for transfers between devices  46.2 us (24%)
  Pallas kernels  40.7 us (21%)
  other arithmetic  17.8 us (9%)
  between operations  14.6 us (8%)
  local copies, waits for them, and re-layouts  10.2 us (5%)
    pallas_call x4, Pallas kernels, call(): pl.pallas_call(kernel, out_shape=[jax.ShapeDtypeStruct(shape, kind) for s...  40.7 us
    ppermute x36, waiting for transfers between devices, swap(): return lax.ppermute(value, PLANE, pairs)  34.6 us
    ppermute x36, starting transfers between devices, swap(): return lax.ppermute(value, PLANE, pairs)  33.3 us
    ppermute x12, starting transfers between devices, shift(): lax.ppermute(value, 'dp', [(i, (i + step) % count) for i in range(count)])  19.2 us
    ppermute x12, waiting for transfers between devices, shift(): lax.ppermute(value, 'dp', [(i, (i + step) % count) for i in range(count)])  8.96 us
    sub x5, other arithmetic, adam_update(): weight - step_rate * (mean_fixed / (jnp.sqrt(var_fixed) + adam_eps) + dec...  4.36 us
  transfers between devices with their start and end apart: 53, of which 24 were waited for; matrix products, arithmetic and copies ran while one was open for 10% of the time, Pallas kernels for 14%

profile of v1, /device:TPU:0, one launch (start us, length us, event | category | flops | bytes accessed | tf_op | source)
XLA Modules:
  0.0 189.0 jit_solution(189202455646307794)
XLA Ops:
  10.3 2.4 %collective-permute-start.2 = (bf16[24,588]{1,0:T(8,128)(2,1)S(1)}, bf16[24,588]{1,0:T(8,128)(2,1)S(1)}, u32[]{:S(2)}, u32[]{:S(2)}) collective-permute-start(bf16[24,588]{1,0:T(8,128)(2,1)S(1)} %get-tuple-element.237), channel_id=1, source_target_pairs={{0,6},{1,7},{2,4},{3,5},{4,2},{5,3},{6,0},{7,1},{8,14},{9,15},{10,... | collective-permute-start | bytes 84680 | tf_op jit(solution)/shard_map/ppermute | solution.py:71
  14.5 2.8 %collective-permute-done.1 = bf16[24,588]{1,0:T(8,128)(2,1)S(1)} collective-permute-done((bf16[24,588]{1,0:T(8,128)(2,1)S(1)}, bf16[24,588]{1,0:T(8,128)(2,1)S(1)}, u32[]{:S(2)}, u32[]{:S(2)}) %collective-permute-start.1) | collective-permute-done | bytes 28256 | tf_op jit(solution)/shard_map/ppermute | solution.py:71
  17.4 3.7 %collective-permute-start.5 = (bf16[4,24,588]{2,1,0:T(8,128)(2,1)S(1)}, bf16[4,24,588]{2,1,0:T(8,128)(2,1)S(1)}, u32[]{:S(2)}, u32[]{:S(2)}) collective-permute-start(bf16[4,24,588]{2,1,0:T(8,128)(2,1)S(1)} %pad_maximum_fusion.9.refs_0_), channel_id=1, source_target_pairs={{0,24},{8,0},{16,8},{24,16},{1,25},{9,1},{17,9},{25,17},{2,26},{10... | collective-permute-start | bytes 338696 | tf_op jit(solution)/shard_map/ppermute | solution.py:76
  22.2 3.4 %all-to-all-start = ((bf16[8,24,384]{2,1,0:T(8,128)(2,1)}), bf16[8,24,384]{2,1,0:T(8,128)(2,1)S(1)}, u32[]{:S(2)}, u32[]{:S(2)}) async-start(bf16[8,24,384]{2,1,0:T(8,128)(2,1)} %reshape.139), calls=%async_computation | async-start | bytes 294912 | tf_op jit(solution)/shard_map/all_to_all | solution.py:522
  26.7 1.9 %collective-permute-start.13 = (bf16[128,768]{1,0:T(8,128)(2,1)S(1)}, bf16[128,768]{1,0:T(8,128)(2,1)S(1)}, u32[]{:S(2)}, u32[]{:S(2)}) collective-permute-start(bf16[128,768]{1,0:T(8,128)(2,1)S(1)} %copy-done.6), channel_id=1, source_target_pairs={{0,1},{1,0},{2,3},{3,2},{4,5},{5,4},{6,7},{7,6},{8,9},{9,8},{10,11... | collective-permute-start | bytes 589832 | tf_op jit(solution)/shard_map/ppermute | solution.py:71
  28.6 1.8 all-to-all-done
  30.5 2.5 %collective-permute-start.7 = (bf16[24,768]{1,0:T(8,128)(2,1)S(1)}, bf16[24,768]{1,0:T(8,128)(2,1)S(1)}, u32[]{:S(2)}, u32[]{:S(2)}) collective-permute-start(bf16[24,768]{1,0:T(8,128)(2,1)S(1)} %convert_element_type.165), channel_id=1, source_target_pairs={{0,16},{8,24},{16,0},{24,8},{1,17},{9,25},{17,1},{25,9},{2,18},{10... | collective-permute-start | bytes 110600 | tf_op jit(solution)/shard_map/ppermute | solution.py:76
  33.0 1.3 collective-permute-start.8
  34.4 2.1 %collective-permute-start.4 = (bf16[4,24,588]{2,1,0:T(8,128)(2,1)S(1)}, bf16[4,24,588]{2,1,0:T(8,128)(2,1)S(1)}, u32[]{:S(2)}, u32[]{:S(2)}) collective-permute-start(bf16[4,24,588]{2,1,0:T(8,128)(2,1)S(1)} %pad_maximum_fusion.9.refs_0_), channel_id=1, source_target_pairs={{0,16},{8,24},{16,0},{24,8},{1,17},{9,25},{17,1},{25,9},{2,18},{10... | collective-permute-start | bytes 338696 | tf_op jit(solution)/shard_map/ppermute | solution.py:76
  38.7 5.3 %collective-permute-done.10.refs_3_ = bf16[4,24,588]{2,1,0:T(8,128)(2,1)S(1)} collective-permute-done((bf16[4,24,588]{2,1,0:T(8,128)(2,1)S(1)}, bf16[4,24,588]{2,1,0:T(8,128)(2,1)S(1)}, u32[]{:S(2)}, u32[]{:S(2)}) %collective-permute-start.10) | collective-permute-done | bytes 112928 | tf_op jit(solution)/shard_map/ppermute | solution.py:71
  44.1 1.1 collective-permute-start.20
  45.3 1.4 collective-permute-start.14
  49.3 1.2 collective-permute-start.12
  51.4 2.0 %collective-permute-done.11.refs_5_ = bf16[4,24,588]{2,1,0:T(8,128)(2,1)S(1)} collective-permute-done((bf16[4,24,588]{2,1,0:T(8,128)(2,1)S(1)}, bf16[4,24,588]{2,1,0:T(8,128)(2,1)S(1)}, u32[]{:S(2)}, u32[]{:S(2)}) %collective-permute-start.11) | collective-permute-done | bytes 112928 | tf_op jit(solution)/shard_map/ppermute | solution.py:71
  53.4 1.3 collective-permute-done.12.refs_7_
  55.4 8.2 %shard_map.296 = (bf16[1024,640]{1,0:T(8,128)(2,1)}, bf16[1024,768]{1,0:T(8,128)(2,1)}, bf16[192,512]{1,0:T(8,128)(2,1)}, f32[4,384,1]{2,1,0:T(8,128)}, bf16[768,640]{1,0:T(8,128)(2,1)}, /*index=5*/f32[12,768]{1,0:T(8,128)}) custom-call(s32[3]{0:T(128)} %pad_add_fusion.place, bf16[4,24,588]{2,1,0:T(8,128)(2,1)} %copy-done.25, ...), custom_call_target="tpu_custom_call" | custom-call | flops 2000000000 | bytes 2476044 | tf_op jit(solution)/shard_map/pallas_call | solution.py:449
  63.7 1.1 collective-permute-start.16
  64.8 1.3 collective-permute-start.17
  66.1 1.1 collective-permute-start.18
  69.8 1.8 collective-permute-done.16
  71.7 2.1 %collective-permute-done.18 = bf16[192,512]{1,0:T(8,128)(2,1)S(1)} collective-permute-done((bf16[192,512]{1,0:T(8,128)(2,1)}, bf16[192,512]{1,0:T(8,128)(2,1)S(1)}, u32[]{:S(2)}, u32[]{:S(2)}) %collective-permute-start.18) | collective-permute-done | bytes 196640 | tf_op jit(solution)/shard_map/ppermute | solution.py:71
  74.6 2.5 %collective-permute-done.22.refs_1_ = bf16[4,4,24,768]{3,2,1,0:T(8,128)(2,1)S(1)} collective-permute-done((bf16[4,4,24,768]{3,2,1,0:T(8,128)(2,1)S(1)}, bf16[4,4,24,768]{3,2,1,0:T(8,128)(2,1)S(1)}, u32[]{:S(2)}, u32[]{:S(2)}) %collective-permute-start.22) | collective-permute-done | bytes 589856 | tf_op jit(solution)/shard_map/ppermute | solution.py:71
  78.2 13.5 %shard_map.297 = (bf16[4,128,768]{2,1,0:T(8,128)(2,1)}, bf16[4,128,768]{2,1,0:T(8,128)(2,1)}, bf16[4,128,768]{2,1,0:T(8,128)(2,1)}, bf16[4,128,768]{2,1,0:T(8,12...) custom-call(s32[3]{0:T(128)} %pad_add_fusion.place, ...), custom_call_target="tpu_custom_call" | custom-call | flops 6000000000 | bytes 7116300 | tf_op jit(solution)/shard_map/pallas_call | solution.py:449
  92.0 2.3 %collective-permute-done.23 = bf16[4,128,768]{2,1,0:T(8,128)(2,1)S(1)} collective-permute-done((bf16[4,128,768]{2,1,0:T(8,128)(2,1)}, bf16[4,128,768]{2,1,0:T(8,128)(2,1)S(1)}, u32[]{:S(2)}, u32[]{:S(2)}) %collective-permute-start.23) | collective-permute-done | bytes 786464 | tf_op jit(solution)/shard_map/ppermute | solution.py:71
  94.3 1.5 add_convert_fusion.2
  96.2 1.3 collective-permute-start.24
  97.5 1.7 collective-permute-start.25
  99.8 1.4 add_convert_fusion.1
  101.1 2.3 %collective-permute-done.24 = bf16[128,768]{1,0:T(8,128)(2,1)S(1)} collective-permute-done((bf16[128,768]{1,0:T(8,128)(2,1)S(1)}, bf16[128,768]{1,0:T(8,128)(2,1)S(1)}, u32[]{:S(2)}, u32[]{:S(2)}) %collective-permute-start.24) | collective-permute-done | bytes 196640 | tf_op jit(solution)/shard_map/ppermute | solution.py:71
  103.4 1.8 collective-permute-done.25
  105.2 3.6 %collective-permute-done.26 = bf16[128,768]{1,0:T(8,128)(2,1)S(1)} collective-permute-done((bf16[128,768]{1,0:T(8,128)(2,1)S(1)}, bf16[128,768]{1,0:T(8,128)(2,1)S(1)}, u32[]{:S(2)}, u32[]{:S(2)}) %collective-permute-start.26) | collective-permute-done | bytes 196640 | tf_op jit(solution)/shard_map/ppermute | solution.py:71
  109.2 1.5 collective-permute-start.28
  110.8 4.6 %collective-permute-done.28.db_far = bf16[128,768]{1,0:T(8,128)(2,1)S(1)} collective-permute-done((bf16[128,768]{1,0:T(8,128)(2,1)S(1)}, bf16[128,768]{1,0:T(8,128)(2,1)S(1)}, u32[]{:S(2)}, u32[]{:S(2)}) %collective-permute-start.28) | collective-permute-done | bytes 196640 | tf_op jit(solution)/shard_map/ppermute | solution.py:71
  115.5 1.3 collective-permute-start.31
  117.6 9.7 %shard_map.298 = (bf16[1024,640]{1,0:T(8,128)(2,1)}, bf16[512,768]{1,0:T(8,128)(2,1)}, bf16[4,4,24,384]{3,2,1,0:T(8,128)(2,1)}, bf16[4,4,24,384]{3,2,1,0:T(8,128)(2,1)}) custom-call(s32[3]{0:T(128)} %pad_add_fusion.place, bf16[128,768]{1,0:T(8,128)(2,1)} %copy-done.23, bf16[128,768]{1,0:T(8,128)(2,1)} %copy-done.35, bf16[128,768]{1,0:T(8,128)(2,1)} %copy-done.36, ...), custom_call_target="tpu_custom_call" | custom-call | flops 10000000000 | bytes 4069388 | tf_op jit(solution)/shard_map/pallas_call | solution.py:449
  127.4 1.7 collective-permute-start.33
  129.2 1.1 collective-permute-start.32
  130.3 9.3 %shard_map.299 = (bf16[4,128,768]{2,1,0:T(8,128)(2,1)}, bf16[4,128,768]{2,1,0:T(8,128)(2,1)}, bf16[4,4,24,448]{3,2,1,0:T(8,128)(2,1)}, bf16[4,4,24,448]{3,2,1,0:T(8,128)(2,1)}) custom-call(s32[3]{0:T(128)} %pad_add_fusion.place, bf16[1024,640]{1,0:T(8,128)(2,1)} %get-tuple-element.131.d_ref, bf16[512,768]{1,0:T(8,128)(2,1)} %get-tuple-element.132.db_all, ...), custom_call_target="tpu_custom_call" | custom-call | flops 6000000000 | bytes 8399372 | tf_op jit(solution)/shard_map/pallas_call | solution.py:449
  142.3 3.9 %collective-permute-start.35 = (bf16[4,24,384]{2,1,0:T(8,128)(2,1)S(1)}, bf16[4,24,384]{2,1,0:T(8,128)(2,1)S(1)}, u32[]{:S(2)}, u32[]{:S(2)}) collective-permute-start(bf16[4,24,384]{2,1,0:T(8,128)(2,1)S(1)} %get-tuple-element.225), channel_id=1, source_target_pairs={{0,16},{8,24},{16,0},{24,8},{1,17},{9,25},{17,1},{25,9},{2,18},{10... | collective-permute-start | bytes 221192 | tf_op jit(solution)/shard_map/ppermute | solution.py:76
  146.2 1.8 fusion.11
  148.8 2.8 %collective-permute-done.35 = bf16[4,24,384]{2,1,0:T(8,128)(2,1)S(1)} collective-permute-done((bf16[4,24,384]{2,1,0:T(8,128)(2,1)S(1)}, bf16[4,24,384]{2,1,0:T(8,128)(2,1)S(1)}, u32[]{:S(2)}, u32[]{:S(2)}) %collective-permute-start.35) | collective-permute-done | bytes 73760 | tf_op jit(solution)/shard_map/ppermute | solution.py:76
  152.5 1.3 collective-permute-start.39
  154.1 1.2 collective-permute-start.42
  156.3 1.4 collective-permute-start.44
  157.7 3.3 %collective-permute-start.40 = (bf16[4,24,448]{2,1,0:T(8,128)(2,1)S(1)}, bf16[4,24,448]{2,1,0:T(8,128)(2,1)S(1)}, u32[]{:S(2)}, u32[]{:S(2)}) collective-permute-start(bf16[4,24,448]{2,1,0:T(8,128)(2,1)S(1)} %get-tuple-element.219), channel_id=1, source_target_pairs={{0,16},{8,24},{16,0},{24,8},{1,17},{9,25},{17,1},{25,9},{2,18},{10... | collective-permute-start | bytes 258056 | tf_op jit(solution)/shard_map/ppermute | solution.py:76
  161.3 4.2 %collective-permute-done.40 = bf16[4,24,448]{2,1,0:T(8,128)(2,1)S(1)} collective-permute-done((bf16[4,24,448]{2,1,0:T(8,128)(2,1)S(1)}, bf16[4,24,448]{2,1,0:T(8,128)(2,1)S(1)}, u32[]{:S(2)}, u32[]{:S(2)}) %collective-permute-start.40) | collective-permute-done | bytes 86048 | tf_op jit(solution)/shard_map/ppermute | solution.py:76
  168.0 3.4 %all-to-all-start.1 = ((bf16[8,24,384]{2,1,0:T(8,128)(2,1)}), bf16[8,24,384]{2,1,0:T(8,128)(2,1)S(1)}, u32[]{:S(2)}, u32[]{:S(2)}) async-start(bf16[8,24,384]{2,1,0:T(8,128)(2,1)} %bitcast.57), calls=%async_computation.2 | async-start | bytes 294912 | tf_op jit(solution)/shard_map/all_to_all | solution.py:712
  171.9 1.7 collective-permute-start.46
  (238 shorter events, 38.3 us)
Async XLA Ops:
  7.2 39.5 %all-gather.5.cloned.1.call-start = ((), (), s32[]{:S(2)}) async-start(), calls=%async_computation.4 | async-start | bytes 1769472 | tf_op jit(solution)/shard_map/all_gather | solution.py:517
  10.3 4.2 %collective-permute-start.2 = (bf16[24,588]{1,0:T(8,128)(2,1)S(1)}, bf16[24,588]{1,0:T(8,128)(2,1)S(1)}, u32[]{:S(2)}, u32[]{:S(2)}) collective-permute-start(bf16[24,588]{1,0:T(8,128)(2,1)S(1)} %get-tuple-element.237), channel_id=1, source_target_pairs={{0,6},{1,7},{2,4},{3,5},{4,2},{5,3},{6,0},{7,1},{8,14},{9,15},{10,... | collective-permute-start | bytes 84680 | tf_op jit(solution)/shard_map/ppermute | solution.py:71
  13.4 3.9 %collective-permute-start.1 = (bf16[24,588]{1,0:T(8,128)(2,1)S(1)}, bf16[24,588]{1,0:T(8,128)(2,1)S(1)}, u32[]{:S(2)}, u32[]{:S(2)}) collective-permute-start(bf16[24,588]{1,0:T(8,128)(2,1)S(1)} %get-tuple-element.236), channel_id=1, source_target_pairs={{0,4},{1,5},{2,6},{3,7},{4,0},{5,1},{6,2},{7,3},{8,12},{9,13},{10,... | collective-permute-start | bytes 84680 | tf_op jit(solution)/shard_map/ppermute | solution.py:71
  17.4 9.3 %collective-permute-start.5 = (bf16[4,24,588]{2,1,0:T(8,128)(2,1)S(1)}, bf16[4,24,588]{2,1,0:T(8,128)(2,1)S(1)}, u32[]{:S(2)}, u32[]{:S(2)}) collective-permute-start(bf16[4,24,588]{2,1,0:T(8,128)(2,1)S(1)} %pad_maximum_fusion.9.refs_0_), channel_id=1, source_target_pairs={{0,24},{8,0},{16,8},{24,16},{1,25},{9,1},{17,9},{25,17},{2,26},{10... | collective-permute-start | bytes 338696 | tf_op jit(solution)/shard_map/ppermute | solution.py:76
  22.2 8.3 %all-to-all-start = ((bf16[8,24,384]{2,1,0:T(8,128)(2,1)}), bf16[8,24,384]{2,1,0:T(8,128)(2,1)S(1)}, u32[]{:S(2)}, u32[]{:S(2)}) async-start(bf16[8,24,384]{2,1,0:T(8,128)(2,1)} %reshape.139), calls=%async_computation | async-start | bytes 294912 | tf_op jit(solution)/shard_map/all_to_all | solution.py:522
  25.5 52.5 %all-gather.7.cloned.1.call-start = ((), (), s32[]{:S(2)}) async-start(), calls=%async_computation.5 | async-start | bytes 1474560 | tf_op jit(solution)/shard_map/all_gather | solution.py:537
  26.6 7.8 %collective-permute-start.3 = (bf16[4,24,588]{2,1,0:T(8,128)(2,1)S(1)}, bf16[4,24,588]{2,1,0:T(8,128)(2,1)S(1)}, u32[]{:S(2)}, u32[]{:S(2)}) collective-permute-start(bf16[4,24,588]{2,1,0:T(8,128)(2,1)S(1)} %pad_maximum_fusion.9.refs_0_), channel_id=1, source_target_pairs={{0,8},{8,16},{16,24},{24,0},{1,9},{9,17},{17,25},{25,1},{2,10},{10... | collective-permute-start | bytes 338696 | tf_op jit(solution)/shard_map/ppermute | solution.py:76
  26.7 18.5 %collective-permute-start.13 = (bf16[128,768]{1,0:T(8,128)(2,1)S(1)}, bf16[128,768]{1,0:T(8,128)(2,1)S(1)}, u32[]{:S(2)}, u32[]{:S(2)}) collective-permute-start(bf16[128,768]{1,0:T(8,128)(2,1)S(1)} %copy-done.6), channel_id=1, source_target_pairs={{0,1},{1,0},{2,3},{3,2},{4,5},{5,4},{6,7},{7,6},{8,9},{9,8},{10,11... | collective-permute-start | bytes 589832 | tf_op jit(solution)/shard_map/ppermute | solution.py:71
  30.5 6.2 %collective-permute-start.6 = (bf16[24,768]{1,0:T(8,128)(2,1)S(1)}, bf16[24,768]{1,0:T(8,128)(2,1)S(1)}, u32[]{:S(2)}, u32[]{:S(2)}) collective-permute-start(bf16[24,768]{1,0:T(8,128)(2,1)S(1)} %convert_element_type.165), channel_id=1, source_target_pairs={{0,8},{8,16},{16,24},{24,0},{1,9},{9,17},{17,25},{25,1},{2,10},{10... | collective-permute-start | bytes 110600 | tf_op jit(solution)/shard_map/ppermute | solution.py:76
  30.5 7.2 %collective-permute-start.7 = (bf16[24,768]{1,0:T(8,128)(2,1)S(1)}, bf16[24,768]{1,0:T(8,128)(2,1)S(1)}, u32[]{:S(2)}, u32[]{:S(2)}) collective-permute-start(bf16[24,768]{1,0:T(8,128)(2,1)S(1)} %convert_element_type.165), channel_id=1, source_target_pairs={{0,16},{8,24},{16,0},{24,8},{1,17},{9,25},{17,1},{25,9},{2,18},{10... | collective-permute-start | bytes 110600 | tf_op jit(solution)/shard_map/ppermute | solution.py:76
  33.0 5.7 %collective-permute-start.8 = (bf16[24,768]{1,0:T(8,128)(2,1)S(1)}, bf16[24,768]{1,0:T(8,128)(2,1)S(1)}, u32[]{:S(2)}, u32[]{:S(2)}) collective-permute-start(bf16[24,768]{1,0:T(8,128)(2,1)S(1)} %convert_element_type.165), channel_id=1, source_target_pairs={{0,24},{8,0},{16,8},{24,16},{1,25},{9,1},{17,9},{25,17},{2,26},{10... | collective-permute-start | bytes 110600 | tf_op jit(solution)/shard_map/ppermute | solution.py:76
  34.4 12.3 %collective-permute-start.4 = (bf16[4,24,588]{2,1,0:T(8,128)(2,1)S(1)}, bf16[4,24,588]{2,1,0:T(8,128)(2,1)S(1)}, u32[]{:S(2)}, u32[]{:S(2)}) collective-permute-start(bf16[4,24,588]{2,1,0:T(8,128)(2,1)S(1)} %pad_maximum_fusion.9.refs_0_), channel_id=1, source_target_pairs={{0,16},{8,24},{16,0},{24,8},{1,17},{9,25},{17,1},{25,9},{2,18},{10... | collective-permute-start | bytes 338696 | tf_op jit(solution)/shard_map/ppermute | solution.py:76
  36.7 10.0 %collective-permute-start.9 = (bf16[4,24,588]{2,1,0:T(8,128)(2,1)S(1)}, bf16[4,24,588]{2,1,0:T(8,128)(2,1)S(1)}, u32[]{:S(2)}, u32[]{:S(2)}) collective-permute-start(bf16[4,24,588]{2,1,0:T(8,128)(2,1)S(1)} %pad_maximum_fusion.9.refs_0_), channel_id=1, source_target_pairs={{0,1},{1,0},{2,3},{3,2},{4,5},{5,4},{6,7},{7,6},{8,9},{9,8},{10,11... | collective-permute-start | bytes 338696 | tf_op jit(solution)/shard_map/ppermute | solution.py:71
  37.7 6.3 %collective-permute-start.10 = (bf16[4,24,588]{2,1,0:T(8,128)(2,1)S(1)}, bf16[4,24,588]{2,1,0:T(8,128)(2,1)S(1)}, u32[]{:S(2)}, u32[]{:S(2)}) collective-permute-start(bf16[4,24,588]{2,1,0:T(8,128)(2,1)S(1)} %collective-permute-done.3.refs_2_), channel_id=1, source_target_pairs={{0,1},{1,0},{2,3},{3,2},{4,5},{5,4},{6,7},{7,6},{8,9},{9,8},{10,11... | collective-permute-start | bytes 338696 | tf_op jit(solution)/shard_map/ppermute | solution.py:71
  44.1 6.4 %collective-permute-start.20 = (bf16[4,24,768]{2,1,0:T(8,128)(2,1)S(1)}, bf16[4,24,768]{2,1,0:T(8,128)(2,1)S(1)}, u32[]{:S(2)}, u32[]{:S(2)}) collective-permute-start(bf16[4,24,768]{2,1,0:T(8,128)(2,1)S(1)} %pad_maximum_fusion.7), channel_id=1, source_target_pairs={{0,1},{1,0},{2,3},{3,2},{4,5},{5,4},{6,7},{7,6},{8,9},{9,8},{10,11... | collective-permute-start | bytes 442376 | tf_op jit(solution)/shard_map/ppermute | solution.py:71
  45.3 18.4 %collective-permute-start.14 = (bf16[2,128,768]{2,1,0:T(8,128)(2,1)S(1)}, bf16[2,128,768]{2,1,0:T(8,128)(2,1)S(1)}, u32[]{:S(2)}, u32[]{:S(2)}) collective-permute-start(bf16[2,128,768]{2,1,0:T(8,128)(2,1)S(1)} %pad_maximum_fusion.2), channel_id=1, source_target_pairs={{0,4},{1,5},{2,6},{3,7},{4,0},{5,1},{6,2},{7,3},{8,12},{9,13},{10,... | collective-permute-start | bytes 1179656 | tf_op jit(solution)/shard_map/ppermute | solution.py:71
  47.5 118.8 %reduce-scatter.2.cloned.1.call-start = ((), (), s32[]{:S(2)}) async-start(), calls=%async_computation.3 | async-start | bytes 1474560 | tf_op jit(solution)/shard_map/reduce_scatter | solution.py:636
  48.4 5.0 %collective-permute-start.11 = (bf16[4,24,588]{2,1,0:T(8,128)(2,1)S(1)}, bf16[4,24,588]{2,1,0:T(8,128)(2,1)S(1)}, u32[]{:S(2)}, u32[]{:S(2)}) collective-permute-start(bf16[4,24,588]{2,1,0:T(8,128)(2,1)S(1)} %collective-permute-done.4.refs_4_), channel_id=1, source_target_pairs={{0,1},{1,0},{2,3},{3,2},{4,5},{5,4},{6,7},{7,6},{8,9},{9,8},{10,11... | collective-permute-start | bytes 338696 | tf_op jit(solution)/shard_map/ppermute | solution.py:71
  49.3 5.5 %collective-permute-start.12 = (bf16[4,24,588]{2,1,0:T(8,128)(2,1)S(1)}, bf16[4,24,588]{2,1,0:T(8,128)(2,1)S(1)}, u32[]{:S(2)}, u32[]{:S(2)}) collective-permute-start(bf16[4,24,588]{2,1,0:T(8,128)(2,1)S(1)} %collective-permute-done.5.refs_6_), channel_id=1, source_target_pairs={{0,1},{1,0},{2,3},{3,2},{4,5},{5,4},{6,7},{7,6},{8,9},{9,8},{10,11... | collective-permute-start | bytes 338696 | tf_op jit(solution)/shard_map/ppermute | solution.py:71
  50.5 23.5 %collective-permute-start.21 = (bf16[2,4,24,768]{3,2,1,0:T(8,128)(2,1)S(1)}, bf16[2,4,24,768]{3,2,1,0:T(8,128)(2,1)S(1)}, u32[]{:S(2)}, u32[]{:S(2)}) collective-permute-start(bf16[2,4,24,768]{3,2,1,0:T(8,128)(2,1)S(1)} %pad_maximum_fusion.3), channel_id=1, source_target_pairs={{0,4},{1,5},{2,6},{3,7},{4,0},{5,1},{6,2},{7,3},{8,12},{9,13},{10,... | collective-permute-start | bytes 884744 | tf_op jit(solution)/shard_map/ppermute | solution.py:71
  63.7 8.0 %collective-permute-start.16 = (bf16[192,512]{1,0:T(8,128)(2,1)}, bf16[192,512]{1,0:T(8,128)(2,1)S(1)}, u32[]{:S(2)}, u32[]{:S(2)}) collective-permute-start(bf16[192,512]{1,0:T(8,128)(2,1)} %get-tuple-element.101), channel_id=1, source_target_pairs={{0,1},{1,0},{2,3},{3,2},{4,5},{5,4},{6,7},{7,6},{8,9},{9,8},{10,11... | collective-permute-start | bytes 589832 | tf_op jit(solution)/shard_map/ppermute | solution.py:71
  64.8 6.9 %collective-permute-start.17 = (bf16[192,512]{1,0:T(8,128)(2,1)}, bf16[192,512]{1,0:T(8,128)(2,1)S(1)}, u32[]{:S(2)}, u32[]{:S(2)}) collective-permute-start(bf16[192,512]{1,0:T(8,128)(2,1)} %get-tuple-element.101), channel_id=1, source_target_pairs={{0,4},{1,5},{2,6},{3,7},{4,0},{5,1},{6,2},{7,3},{8,12},{9,13},{10,... | collective-permute-start | bytes 589832 | tf_op jit(solution)/shard_map/ppermute | solution.py:71
  66.1 7.7 %collective-permute-start.18 = (bf16[192,512]{1,0:T(8,128)(2,1)}, bf16[192,512]{1,0:T(8,128)(2,1)S(1)}, u32[]{:S(2)}, u32[]{:S(2)}) collective-permute-start(bf16[192,512]{1,0:T(8,128)(2,1)} %get-tuple-element.101), channel_id=1, source_target_pairs={{0,5},{1,4},{2,7},{3,6},{4,1},{5,0},{6,3},{7,2},{8,13},{9,12},{10,... | collective-permute-start | bytes 589832 | tf_op jit(solution)/shard_map/ppermute | solution.py:71
  68.8 8.3 %collective-permute-start.15 = (bf16[4,128,768]{2,1,0:T(8,128)(2,1)S(1)}, bf16[4,128,768]{2,1,0:T(8,128)(2,1)S(1)}, u32[]{:S(2)}, u32[]{:S(2)}) collective-permute-start(bf16[4,128,768]{2,1,0:T(8,128)(2,1)S(1)} %constant_dynamic-update-slice_fusion.cot_a), channel_id=1, source_target_pairs={{0,2},{1,3},{2,0},{3,1},{4,6},{5,7},{6,4},{7,5},{8,10},{9,11},{10,... | collective-permute-start | bytes 2359304 | tf_op jit(solution)/shard_map/ppermute | solution.py:71
  73.9 4.2 %collective-permute-start.19 = (bf16[4,192,512]{2,1,0:T(8,128)(2,1)S(1)}, bf16[4,192,512]{2,1,0:T(8,128)(2,1)}, u32[]{:S(2)}, u32[]{:S(2)}) collective-permute-start(bf16[4,192,512]{2,1,0:T(8,128)(2,1)S(1)} %pad_maximum_fusion.att_a), channel_id=1, source_target_pairs={{0,2},{1,3},{2,0},{3,1},{4,6},{5,7},{6,4},{7,5},{8,10},{9,11},{10,... | collective-permute-start | bytes 2359304 | tf_op jit(solution)/shard_map/ppermute | solution.py:71
  95.8 4.0 %collective-permute-start.27 = (bf16[4,128,768]{2,1,0:T(8,128)(2,1)}, bf16[4,128,768]{2,1,0:T(8,128)(2,1)}, u32[]{:S(2)}, u32[]{:S(2)}) collective-permute-start(bf16[4,128,768]{2,1,0:T(8,128)(2,1)} %get-tuple-element.111), channel_id=1, source_target_pairs={{0,2},{1,3},{2,0},{3,1},{4,6},{5,7},{6,4},{7,5},{8,10},{9,11},{10,... | collective-permute-start | bytes 2359304 | tf_op jit(solution)/shard_map/ppermute | solution.py:71
  96.2 7.2 %collective-permute-start.24 = (bf16[128,768]{1,0:T(8,128)(2,1)S(1)}, bf16[128,768]{1,0:T(8,128)(2,1)S(1)}, u32[]{:S(2)}, u32[]{:S(2)}) collective-permute-start(bf16[128,768]{1,0:T(8,128)(2,1)S(1)} %get-tuple-element.216), channel_id=1, source_target_pairs={{0,1},{1,0},{2,3},{3,2},{4,5},{5,4},{6,7},{7,6},{8,9},{9,8},{10,11... | collective-permute-start | bytes 589832 | tf_op jit(solution)/shard_map/ppermute | solution.py:71
  97.5 7.8 %collective-permute-start.25 = (bf16[128,768]{1,0:T(8,128)(2,1)S(1)}, bf16[128,768]{1,0:T(8,128)(2,1)S(1)}, u32[]{:S(2)}, u32[]{:S(2)}) collective-permute-start(bf16[128,768]{1,0:T(8,128)(2,1)S(1)} %get-tuple-element.215), channel_id=1, source_target_pairs={{0,4},{1,5},{2,6},{3,7},{4,0},{5,1},{6,2},{7,3},{8,12},{9,13},{10,... | collective-permute-start | bytes 589832 | tf_op jit(solution)/shard_map/ppermute | solution.py:71
  99.1 9.7 %collective-permute-start.26 = (bf16[128,768]{1,0:T(8,128)(2,1)S(1)}, bf16[128,768]{1,0:T(8,128)(2,1)S(1)}, u32[]{:S(2)}, u32[]{:S(2)}) collective-permute-start(bf16[128,768]{1,0:T(8,128)(2,1)S(1)} %get-tuple-element.214), channel_id=1, source_target_pairs={{0,5},{1,4},{2,7},{3,6},{4,1},{5,0},{6,3},{7,2},{8,13},{9,12},{10,... | collective-permute-start | bytes 589832 | tf_op jit(solution)/shard_map/ppermute | solution.py:71
  109.2 6.1 %collective-permute-start.28 = (bf16[128,768]{1,0:T(8,128)(2,1)S(1)}, bf16[128,768]{1,0:T(8,128)(2,1)S(1)}, u32[]{:S(2)}, u32[]{:S(2)}) collective-permute-start(bf16[128,768]{1,0:T(8,128)(2,1)S(1)} %get-tuple-element.207.db_own), channel_id=1, source_target_pairs={{0,4},{1,5},{2,6},{3,7},{4,0},{5,1},{6,2},{7,3},{8,12},{9,13},{10,... | collective-permute-start | bytes 589832 | tf_op jit(solution)/shard_map/ppermute | solution.py:71
  110.8 6.1 %collective-permute-start.29 = (bf16[128,768]{1,0:T(8,128)(2,1)S(1)}, bf16[128,768]{1,0:T(8,128)(2,1)S(1)}, u32[]{:S(2)}, u32[]{:S(2)}) collective-permute-start(bf16[128,768]{1,0:T(8,128)(2,1)S(1)} %get-tuple-element.207.db_own), channel_id=1, source_target_pairs={{0,2},{1,3},{2,0},{3,1},{4,6},{5,7},{6,4},{7,5},{8,10},{9,11},{10,... | collective-permute-start | bytes 589832 | tf_op jit(solution)/shard_map/ppermute | solution.py:71
  115.5 11.8 %collective-permute-start.31 = (bf16[2,128,768]{2,1,0:T(8,128)(2,1)S(1)}, bf16[2,128,768]{2,1,0:T(8,128)(2,1)S(1)}, u32[]{:S(2)}, u32[]{:S(2)}) collective-permute-start(bf16[2,128,768]{2,1,0:T(8,128)(2,1)S(1)} %slice.92), channel_id=1, source_target_pairs={{0,1},{1,0},{2,3},{3,2},{4,5},{5,4},{6,7},{7,6},{8,9},{9,8},{10,11... | collective-permute-start | bytes 1179656 | tf_op jit(solution)/shard_map/ppermute | solution.py:71
  127.4 12.2 %collective-permute-start.33 = (bf16[128,768]{1,0:T(8,128)(2,1)S(1)}, bf16[128,768]{1,0:T(8,128)(2,1)S(1)}, u32[]{:S(2)}, u32[]{:S(2)}) collective-permute-start(bf16[128,768]{1,0:T(8,128)(2,1)S(1)} %slice_bitcast_fusion.4), channel_id=1, source_target_pairs={{0,4},{1,5},{2,6},{3,7},{4,0},{5,1},{6,2},{7,3},{8,12},{9,13},{10,... | collective-permute-start | bytes 589832 | tf_op jit(solution)/shard_map/ppermute | solution.py:71
  129.2 10.4 %collective-permute-start.32 = (bf16[4,4,24,384]{3,2,1,0:T(8,128)(2,1)S(1)}, bf16[4,4,24,384]{3,2,1,0:T(8,128)(2,1)S(1)}, u32[]{:S(2)}, u32[]{:S(2)}) collective-permute-start(bf16[4,4,24,384]{3,2,1,0:T(8,128)(2,1)S(1)} %copy-done.34), channel_id=1, source_target_pairs={{0,1},{1,0},{2,3},{3,2},{4,5},{5,4},{6,7},{7,6},{8,9},{9,8},{10,11... | collective-permute-start | bytes 884744 | tf_op jit(solution)/shard_map/ppermute | solution.py:71
  140.3 12.0 %collective-permute-start.38 = (bf16[4,128,768]{2,1,0:T(8,128)(2,1)}, bf16[4,128,768]{2,1,0:T(8,128)(2,1)S(1)}, u32[]{:S(2)}, u32[]{:S(2)}) collective-permute-start(bf16[4,128,768]{2,1,0:T(8,128)(2,1)} %get-tuple-element.147), channel_id=1, source_target_pairs={{0,2},{1,3},{2,0},{3,1},{4,6},{5,7},{6,4},{7,5},{8,10},{9,11},{10,... | collective-permute-start | bytes 2359304 | tf_op jit(solution)/shard_map/ppermute | solution.py:71
  140.6 11.8 %collective-permute-start.37 = (bf16[4,4,24,448]{3,2,1,0:T(8,128)(2,1)}, bf16[4,4,24,448]{3,2,1,0:T(8,128)(2,1)S(1)}, u32[]{:S(2)}, u32[]{:S(2)}) collective-permute-start(bf16[4,4,24,448]{3,2,1,0:T(8,128)(2,1)} %get-tuple-element.145), channel_id=1, source_target_pairs={{0,1},{1,0},{2,3},{3,2},{4,5},{5,4},{6,7},{7,6},{8,9},{9,8},{10,11... | collective-permute-start | bytes 1032200 | tf_op jit(solution)/shard_map/ppermute | solution.py:71
  141.6 7.2 %collective-permute-start.34 = (bf16[4,24,384]{2,1,0:T(8,128)(2,1)S(1)}, bf16[4,24,384]{2,1,0:T(8,128)(2,1)S(1)}, u32[]{:S(2)}, u32[]{:S(2)}) collective-permute-start(bf16[4,24,384]{2,1,0:T(8,128)(2,1)S(1)} %get-tuple-element.226), channel_id=1, source_target_pairs={{0,8},{8,16},{16,24},{24,0},{1,9},{9,17},{17,25},{25,1},{2,10},{10... | collective-permute-start | bytes 221192 | tf_op jit(solution)/shard_map/ppermute | solution.py:76
  142.3 9.3 %collective-permute-start.35 = (bf16[4,24,384]{2,1,0:T(8,128)(2,1)S(1)}, bf16[4,24,384]{2,1,0:T(8,128)(2,1)S(1)}, u32[]{:S(2)}, u32[]{:S(2)}) collective-permute-start(bf16[4,24,384]{2,1,0:T(8,128)(2,1)S(1)} %get-tuple-element.225), channel_id=1, source_target_pairs={{0,16},{8,24},{16,0},{24,8},{1,17},{9,25},{17,1},{25,9},{2,18},{10... | collective-permute-start | bytes 221192 | tf_op jit(solution)/shard_map/ppermute | solution.py:76
  146.2 5.8 %collective-permute-start.36 = (bf16[4,24,384]{2,1,0:T(8,128)(2,1)S(1)}, bf16[4,24,384]{2,1,0:T(8,128)(2,1)S(1)}, u32[]{:S(2)}, u32[]{:S(2)}) collective-permute-start(bf16[4,24,384]{2,1,0:T(8,128)(2,1)S(1)} %get-tuple-element.224), channel_id=1, source_target_pairs={{0,24},{8,0},{16,8},{24,16},{1,25},{9,1},{17,9},{25,17},{2,26},{10... | collective-permute-start | bytes 221192 | tf_op jit(solution)/shard_map/ppermute | solution.py:76
  152.5 8.5 %collective-permute-start.39 = (bf16[4,24,448]{2,1,0:T(8,128)(2,1)S(1)}, bf16[4,24,448]{2,1,0:T(8,128)(2,1)S(1)}, u32[]{:S(2)}, u32[]{:S(2)}) collective-permute-start(bf16[4,24,448]{2,1,0:T(8,128)(2,1)S(1)} %get-tuple-element.220), channel_id=1, source_target_pairs={{0,8},{8,16},{16,24},{24,0},{1,9},{9,17},{17,25},{25,1},{2,10},{10... | collective-permute-start | bytes 258056 | tf_op jit(solution)/shard_map/ppermute | solution.py:76
  154.1 12.0 %collective-permute-start.42 = (bf16[128,768]{1,0:T(8,128)(2,1)S(1)}, bf16[128,768]{1,0:T(8,128)(2,1)S(1)}, u32[]{:S(2)}, u32[]{:S(2)}) collective-permute-start(bf16[128,768]{1,0:T(8,128)(2,1)S(1)} %get-tuple-element.212), channel_id=1, source_target_pairs={{0,1},{1,0},{2,3},{3,2},{4,5},{5,4},{6,7},{7,6},{8,9},{9,8},{10,11... | collective-permute-start | bytes 589832 | tf_op jit(solution)/shard_map/ppermute | solution.py:71
  155.3 10.7 %collective-permute-start.43 = (bf16[128,768]{1,0:T(8,128)(2,1)S(1)}, bf16[128,768]{1,0:T(8,128)(2,1)S(1)}, u32[]{:S(2)}, u32[]{:S(2)}) collective-permute-start(bf16[128,768]{1,0:T(8,128)(2,1)S(1)} %get-tuple-element.211), channel_id=1, source_target_pairs={{0,4},{1,5},{2,6},{3,7},{4,0},{5,1},{6,2},{7,3},{8,12},{9,13},{10,... | collective-permute-start | bytes 589832 | tf_op jit(solution)/shard_map/ppermute | solution.py:71
  156.3 9.8 %collective-permute-start.44 = (bf16[128,768]{1,0:T(8,128)(2,1)S(1)}, bf16[128,768]{1,0:T(8,128)(2,1)S(1)}, u32[]{:S(2)}, u32[]{:S(2)}) collective-permute-start(bf16[128,768]{1,0:T(8,128)(2,1)S(1)} %get-tuple-element.210), channel_id=1, source_target_pairs={{0,5},{1,4},{2,7},{3,6},{4,1},{5,0},{6,3},{7,2},{8,13},{9,12},{10,... | collective-permute-start | bytes 589832 | tf_op jit(solution)/shard_map/ppermute | solution.py:71
  157.7 7.8 %collective-permute-start.40 = (bf16[4,24,448]{2,1,0:T(8,128)(2,1)S(1)}, bf16[4,24,448]{2,1,0:T(8,128)(2,1)S(1)}, u32[]{:S(2)}, u32[]{:S(2)}) collective-permute-start(bf16[4,24,448]{2,1,0:T(8,128)(2,1)S(1)} %get-tuple-element.219), channel_id=1, source_target_pairs={{0,16},{8,24},{16,0},{24,8},{1,17},{9,25},{17,1},{25,9},{2,18},{10... | collective-permute-start | bytes 258056 | tf_op jit(solution)/shard_map/ppermute | solution.py:76
  161.0 5.1 %collective-permute-start.41 = (bf16[4,24,448]{2,1,0:T(8,128)(2,1)S(1)}, bf16[4,24,448]{2,1,0:T(8,128)(2,1)S(1)}, u32[]{:S(2)}, u32[]{:S(2)}) collective-permute-start(bf16[4,24,448]{2,1,0:T(8,128)(2,1)S(1)} %get-tuple-element.218), channel_id=1, source_target_pairs={{0,24},{8,0},{16,8},{24,16},{1,25},{9,1},{17,9},{25,17},{2,26},{10... | collective-permute-start | bytes 258056 | tf_op jit(solution)/shard_map/ppermute | solution.py:76
  168.0 12.7 %all-to-all-start.1 = ((bf16[8,24,384]{2,1,0:T(8,128)(2,1)}), bf16[8,24,384]{2,1,0:T(8,128)(2,1)S(1)}, u32[]{:S(2)}, u32[]{:S(2)}) async-start(bf16[8,24,384]{2,1,0:T(8,128)(2,1)} %bitcast.57), calls=%async_computation.2 | async-start | bytes 294912 | tf_op jit(solution)/shard_map/all_to_all | solution.py:712
  171.4 5.3 %collective-permute-start.45 = (bf16[24,588]{1,0:T(8,128)(2,1)S(1)}, bf16[24,588]{1,0:T(8,128)(2,1)S(1)}, u32[]{:S(2)}, u32[]{:S(2)}) collective-permute-start(bf16[24,588]{1,0:T(8,128)(2,1)S(1)} %get-tuple-element.239), channel_id=1, source_target_pairs={{0,2},{1,3},{2,0},{3,1},{4,6},{5,7},{6,4},{7,5},{8,10},{9,11},{10,... | collective-permute-start | bytes 84680 | tf_op jit(solution)/shard_map/ppermute | solution.py:71
  171.9 5.0 %collective-permute-start.46 = (bf16[24,588]{1,0:T(8,128)(2,1)S(1)}, bf16[24,588]{1,0:T(8,128)(2,1)S(1)}, u32[]{:S(2)}, u32[]{:S(2)}) collective-permute-start(bf16[24,588]{1,0:T(8,128)(2,1)S(1)} %get-tuple-element.240), channel_id=1, source_target_pairs={{0,4},{1,5},{2,6},{3,7},{4,0},{5,1},{6,2},{7,3},{8,12},{9,13},{10,... | collective-permute-start | bytes 84680 | tf_op jit(solution)/shard_map/ppermute | solution.py:71
  (50 other events, 328.0 us)
Sparse Core Ops, SparseCore 0:
  9.9 30.7 all-gather.4
  47.6 30.1 all-gather.6
  115.6 30.9 reduce-scatter.1
